TPU v7x, 512 devices: a whole 4x4x16 slice. The times are simulated.
512 devices in a mesh: tile: 128 (over z, y, core), head: 4 (over x).
Axes of the slice: x: 4, y: 4, z: 16, core: 2. Of those that a mesh axis runs over, the one named last changes fastest.
Arguments:
- grid_tokens: bfloat16 [65536, 768], P('tile')
- obs_tokens: bfloat16 [65536, 768], P('tile')
- w_query: bfloat16 [768, 768], P(None, 'head'), may hold values from -0.21875 to 0.21875
- w_gridval: bfloat16 [768, 768], P(None, 'head'), may hold values from -0.21875 to 0.21875
- w_key: bfloat16 [768, 768], P(None, 'head'), may hold values from -0.21875 to 0.21875
- w_obsval: bfloat16 [768, 768], P(None, 'head'), may hold values from -0.21875 to 0.21875
- w_gridout: bfloat16 [768, 768], P('head'), may hold values from -0.21875 to 0.21875
- w_obsout: bfloat16 [768, 768], P('head'), may hold values from -0.21875 to 0.21875
- obs_count: int32 [128], P('tile'), may hold values from 1 to 2, as said below
- home_block: int32 [256], P('tile'), may hold values from 0 to 1
- seam_block: int32 [256], P('tile'), may hold values from 0 to 3, as said below
Outputs:
- grid_out: bfloat16 [65536, 768], P(('tile', 'head'))
- obs_out: bfloat16 [65536, 768], P(('tile', 'head'))
Inputs may be any that keep to these rules, and one draw needn't show every extreme that they name: `obs_count`: every tile has at least one live slot; some tile has all 2 slots live in every draw. `seam_block`: slot 0 of every tile pairs with a block of the previous tile and slot 1 with a block of the next tile; other slots either way.
All inputs are finite; a program needn't handle non-finite values.
Results may differ from a plain program's by a relative error of at most 0.018.
The roundings to bfloat16 on the way count: a program that leaves them out, or rounds other values in their place, can miss the bound.
Values may be sent and summed in bfloat16 or wider, within the bound.
No kernel may reach another device: no remote copies, remote signals or barrier semaphores. Data moves between devices by JAX's collectives and lax.ppermute only.
A program may use at most 64 MiB of HBM per device.

v0:
```python
import jax
import jax.numpy as jnp
from jax import lax
from jax.sharding import PartitionSpec as P

HD = 64
BS = 256


NEG = -1e30


def with_halo(shard, sides, width):
    for axis, dim in sides:
        count, length = (lax.axis_size(axis), shard.shape[dim])
        up = [(i, (i + 1) % count) for i in range(count)]
        down = [(j, i) for i, j in up]
        last = lax.slice_in_dim(shard, length - width, length, axis=dim)
        leading = lax.slice_in_dim(shard, 0, width, axis=dim)
        before = lax.ppermute(last, axis, up)
        after = lax.ppermute(leading, axis, down)
        shard = jnp.concatenate([before, shard, after], axis=dim)
    return shard


def shifted(value, axis, steps):
    count = lax.axis_size(axis)
    pairs = [(source, (source + steps) % count) for source in range(count)]
    return lax.ppermute(value, axis, pairs)


def pair_stats(q, k, vgrid, vobs):
    s = jnp.einsum("ihd,jhd->hij", q, k, preferred_element_type=jnp.float32) / HD**0.5
    mg = jnp.max(s, axis=2)
    eg = jnp.exp(s - mg[:, :, None]).astype(jnp.bfloat16)
    lg = jnp.sum(eg.astype(jnp.float32), axis=2)
    ag = jnp.einsum("hij,jhd->ihd", eg, vobs, preferred_element_type=jnp.float32)
    mo = jnp.max(s, axis=1)
    eo = jnp.exp(s - mo[:, None, :]).astype(jnp.bfloat16)
    lo = jnp.sum(eo.astype(jnp.float32), axis=1)
    ao = jnp.einsum("hij,ihd->jhd", eo, vgrid, preferred_element_type=jnp.float32)
    return (mg, lg, ag, mo, lo, ao)


def combine_three(parts):
    top = jnp.maximum(jnp.maximum(parts[0][0], parts[1][0]), parts[2][0])
    l_sum = jnp.zeros_like(top)
    a_sum = jnp.zeros_like(parts[0][2])
    for m_part, l_part, a_part in parts:
        scale = jnp.exp(m_part - top)
        l_sum = l_sum + scale * l_part
        a_sum = a_sum + jnp.transpose(scale, (0, 2, 1))[..., None] * a_part
    l_safe = jnp.where(l_sum > 0, l_sum, 1.0)
    return a_sum / jnp.transpose(l_safe, (0, 2, 1))[..., None]


def block_fold(targets, counting, count_blocks, mg, lg, ag):
    onehot = (targets[:, None] == jnp.arange(count_blocks, dtype=jnp.int32)[None, :]) & counting[
        :, None
    ]
    m_ext = jnp.max(jnp.where(onehot[:, :, None, None], mg[:, None], NEG), axis=0)
    weight = jnp.where(onehot[:, :, None, None], jnp.exp(mg[:, None] - m_ext[None]), 0.0)
    l_ext = jnp.einsum("pehi,phi->ehi", weight, lg)
    a_ext = jnp.einsum("pehi,pihd->eihd", weight, ag)
    return (m_ext, l_ext, a_ext)


def obs_fold(home, seam, live, rows_obs, width):
    m_obs = jnp.maximum(home[0], seam[0])
    w_home = jnp.exp(home[0] - m_obs)
    w_seam = jnp.exp(seam[0] - m_obs)
    l_obs = w_home * home[1] + w_seam * seam[1]
    a_obs = (
        jnp.transpose(w_home, (0, 2, 1))[..., None] * home[2]
        + jnp.transpose(w_seam, (0, 2, 1))[..., None] * seam[2]
    )
    obs_mix = a_obs / jnp.transpose(l_obs, (0, 2, 1))[..., None]
    return (
        jnp.where(live[:, None, None, None], obs_mix, 0.0)
        .astype(jnp.bfloat16)
        .reshape(rows_obs, width)
    )


def body(
    grid_tokens,
    obs_tokens,
    w_query,
    w_gridval,
    w_key,
    w_obsval,
    w_gridout,
    w_obsout,
    obs_count,
    home_block,
    seam_block,
):
    rows_grid = grid_tokens.shape[0]
    rows_obs = obs_tokens.shape[0]
    blocks = rows_grid // BS
    slots = rows_obs // BS
    width = w_query.shape[1]
    heads_dev = width // HD
    query = jnp.dot(grid_tokens, w_query, preferred_element_type=jnp.float32).astype(jnp.bfloat16)
    grid_value = jnp.dot(grid_tokens, w_gridval, preferred_element_type=jnp.float32).astype(
        jnp.bfloat16
    )
    key_flat = jnp.dot(obs_tokens, w_key, preferred_element_type=jnp.float32).astype(jnp.bfloat16)
    value_flat = jnp.dot(obs_tokens, w_obsval, preferred_element_type=jnp.float32).astype(
        jnp.bfloat16
    )
    slot_ids = jnp.arange(slots, dtype=jnp.int32)
    live = slot_ids < obs_count[0]
    key = key_flat.reshape(slots, BS, heads_dev, HD)
    obs_value = value_flat.reshape(slots, BS, heads_dev, HD)
    widened = with_halo(jnp.stack([query, grid_value]), (("tile", 1),), rows_grid)
    wide_query = widened[0].reshape(3 * blocks, BS, heads_dev, HD)
    wide_value = widened[1].reshape(3 * blocks, BS, heads_dev, HD)
    home_ext = blocks + home_block
    seam_ext = jnp.where(seam_block < blocks, seam_block, seam_block + blocks)
    targets = jnp.concatenate([home_ext, seam_ext])
    sources = jnp.concatenate([slot_ids, slot_ids])
    live_pair = jnp.concatenate([live, live])
    mg, lg, ag, mo, lo, ao = jax.vmap(pair_stats)(
        wide_query[targets], key[sources], wide_value[targets], obs_value[sources]
    )
    obs_mix = obs_fold(
        (mo[:slots], lo[:slots], ao[:slots]),
        (mo[slots:], lo[slots:], ao[slots:]),
        live,
        rows_obs,
        width,
    )
    m_ext, l_ext, a_ext = block_fold(targets, live_pair, 3 * blocks, mg, lg, ag)
    lower_part = (m_ext[:blocks], l_ext[:blocks], a_ext[:blocks])
    upper_part = (m_ext[2 * blocks :], l_ext[2 * blocks :], a_ext[2 * blocks :])
    own_part = (m_ext[blocks : 2 * blocks], l_ext[blocks : 2 * blocks], a_ext[blocks : 2 * blocks])
    above = shifted((lower_part[0], lower_part[1], lower_part[2]), "tile", -1)
    below = shifted((upper_part[0], upper_part[1], upper_part[2]), "tile", 1)
    grid_mix = (
        combine_three((own_part, above, below)).astype(jnp.bfloat16).reshape(rows_grid, width)
    )
    groups = lax.axis_size("head")
    full_grid_w, full_obs_w = (
        lax.all_gather(w_gridout, "head", axis=0, tiled=True),
        lax.all_gather(w_obsout, "head", axis=0, tiled=True),
    )
    grid_rows, obs_rows = (
        lax.all_to_all(grid_mix, "head", split_axis=0, concat_axis=1, tiled=True),
        lax.all_to_all(obs_mix, "head", split_axis=0, concat_axis=1, tiled=True),
    )

    def apply_out(rows, weight_full):
        total = jnp.zeros((rows.shape[0], weight_full.shape[1]), jnp.float32)
        for group in range(groups):
            piece = jnp.dot(
                rows[:, group * width : (group + 1) * width],
                weight_full[group * width : (group + 1) * width],
                preferred_element_type=jnp.float32,
            )
            total = total + piece.astype(jnp.bfloat16).astype(jnp.float32)
        return total.astype(jnp.bfloat16)

    grid_out = apply_out(grid_rows, full_grid_w)
    obs_out = apply_out(obs_rows, full_obs_w)
    return (grid_out, obs_out)


def solution(mesh):
    return jax.shard_map(
        body,
        mesh=mesh,
        in_specs=(
            P("tile", None),
            P("tile", None),
            P(None, "head"),
            P(None, "head"),
            P(None, "head"),
            P(None, "head"),
            P("head", None),
            P("head", None),
            P("tile"),
            P("tile"),
            P("tile"),
        ),
        out_specs=(P(("tile", "head"), None), P(("tile", "head"), None)),
        check_vma=False,
    )
```

profile of v0, /device:TPU:1, one launch (start us, length us, event | category | flops | bytes accessed | tf_op | source)
XLA Modules:
  0.0 122.6 jit_solution(11880298327473566152)
XLA Ops:
  7.2 0.7 all-gather.5.cloned.1.call-update
  8.3 1.4 %fusion.18 = bf16[1,512,192]{1,2,0:T(8,128)(2,1)S(1)} fusion(bf16[512,768]{1,0:T(8,128)(2,1)S(1)} %copy-done, bf16[768,192]{0,1:T(8,128)(2,1)} %param.13), kind=kOutput, calls=%fused_computation.46 | convolution fusion | flops 151093248 | bytes 1277952 | tf_op jit(solution)/shard_map/dot_general | solution.py:104
  10.2 8.8 %collective-permute-start.1 = (bf16[2,512,192]{1,2,0:T(8,128)(2,1)S(1)}, bf16[2,512,192]{1,2,0:T(8,128)(2,1)S(1)}, u32[]{:S(2)}, u32[]{:S(2)}) collective-permute-start(bf16[2,512,192]{1,2,0:T(8,128)(2,1)S(1)} %pad_maximum_fusion.1), channel_id=1, source_target_pairs={{4,0},{8,4},{12,8},{16,12},{20,16},{24,20},{28,24},{32,28},{36,32}... | collective-permute-start | bytes 1179656 | tf_op jit(solution)/shard_map/ppermute | solution.py:21
  19.0 1.9 %collective-permute-start = (bf16[2,512,192]{1,2,0:T(8,128)(2,1)S(1)}, bf16[2,512,192]{1,2,0:T(8,128)(2,1)S(1)}, u32[]{:S(2)}, u32[]{:S(2)}) collective-permute-start(bf16[2,512,192]{1,2,0:T(8,128)(2,1)S(1)} %pad_maximum_fusion.1), channel_id=1, source_target_pairs={{0,4},{4,8},{8,12},{12,16},{16,20},{20,24},{24,28},{28,32},{32,36}... | collective-permute-start | bytes 1179656 | tf_op jit(solution)/shard_map/ppermute | solution.py:20
  21.7 1.4 %convolution_convert_fusion.9 = bf16[512,192]{0,1:T(8,128)(2,1)S(1)} fusion(bf16[512,768]{1,0:T(8,128)(2,1)S(1)} %copy-done.2, bf16[768,192]{0,1:T(8,128)(2,1)} %param.15), kind=kOutput, calls=%fused_computation.43 | convolution fusion | flops 151093248 | bytes 1277952 | tf_op jit(solution)/shard_map/dot_general | solution.py:108
  23.2 1.4 %convolution_convert_fusion.8 = bf16[512,192]{0,1:T(8,128)(2,1)S(1)} fusion(bf16[512,768]{1,0:T(8,128)(2,1)S(1)} %copy-done.2, bf16[768,192]{0,1:T(8,128)(2,1)} %param.16), kind=kOutput, calls=%fused_computation.42 | convolution fusion | flops 151093248 | bytes 1277952 | tf_op jit(solution)/shard_map/dot_general | solution.py:109
  24.7 0.6 gather_fusion.1
  26.2 1.9 %collective-permute-done = bf16[2,512,192]{1,2,0:T(8,128)(2,1)S(1)} collective-permute-done((bf16[2,512,192]{1,2,0:T(8,128)(2,1)S(1)}, bf16[2,512,192]{1,2,0:T(8,128)(2,1)S(1)}, u32[]{:S(2)}, u32[]{:S(2)}) %collective-permute-start) | collective-permute-done | bytes 393248 | tf_op jit(solution)/shard_map/ppermute | solution.py:20
  28.2 0.9 fusion.64
  29.1 0.6 reshape_squeeze.7
  29.9 2.4 %reshape_squeeze.6 = bf16[6,256,3,64]{1,0,3,2:T(8,128)(2,1)} reshape(bf16[1,1536,192]{1,2,0:T(8,128)(2,1)} %get-tuple-element.9) | data formatting | bytes 1179648 | tf_op jit(solution)/shard_map/reshape;squeeze | solution.py:117
  32.3 1.3 %copy.51 = bf16[6,256,3,64]{1,3,2,0:T(8,128)(2,1)S(1)} copy(bf16[6,256,3,64]{1,0,3,2:T(8,128)(2,1)} %reshape_squeeze.6) | data formatting | bytes 1179648 | tf_op jit(solution)/shard_map/reshape;squeeze | solution.py:117
  34.7 2.3 %multiply_reduce_fusion = (f32[4,3,256]{2,1,0:T(4,128)S(1)}, f32[4,3,256]{2,1,0:T(4,128)S(1)}, f32[4,3,256,256]{3,2,1,0:T(8,128)}) fusion(bf16[4,256,3,64]{1,3,2,0:T(8,128)(2,1)S(1)} %gather_fusion, bf16[4,256,3,64]{1,3,2,0:T(8,128)(2,1)S(1)} %gather_fusion.1), kind=kOutput, calls=%fused_computation.8 | convolution fusion | flops 103016448 | bytes 3956736 | tf_op jit(solution)/shard_map/vmap(ihd,jhd->hij)/dot_general | solution.py:33
  37.3 2.8 %convolution_bitcast_fusion.1 = bf16[4,256,3,64]{1,3,2,0:T(8,128)(2,1)S(1)} fusion(bf16[4,256,3,64]{1,3,2,0:T(8,128)(2,1)S(1)} %gather_fusion.2, f32[4,3,256,256]{3,2,1,0:T(8,128)} %get-tuple-element.26, f32[4,3,256]{2,1,0:T(4,128)S(1)} %get-tuple-element.5), kind=kOutput, calls=%fused_computation.16 | convolution fusion | flops 103022592 | bytes 3944448 | tf_op jit(solution)/shard_map/vmap(hij,jhd->ihd)/dot_general | solution.py:37
  40.2 1.7 %convert_reduce_fusion = (f32[4,3,256]{2,1,0:T(4,128)S(1)}, bf16[4,3,256]{2,1,0:T(4,128)(2,1)S(1)}) fusion(f32[4,3,256]{2,1,0:T(4,128)S(1)} %get-tuple-element.4, f32[4,3,256,256]{3,2,1,0:T(8,128)S(1)} %copy-done.1, f32[4,3,256]{2,1,0:T(4,128)S(1)} %get-tuple-element.5), kind=kLoop, calls=%fused_computation.4 | loop fusion | flops 7071744 | bytes 3188736 | tf_op jit(solution)/shard_map/vmap()/reduce_sum | solution.py:40
  41.9 0.7 convolution_bitcast_fusion
  43.1 0.7 copy.65
  43.8 4.0 %all-to-all-start.1 = ((bf16[4,128,192]{1,2,0:T(8,128)(2,1)}), bf16[4,128,192]{1,2,0:T(8,128)(2,1)}, u32[]{:S(2)}, u32[]{:S(2)}) async-start(bf16[4,128,192]{1,2,0:T(8,128)(2,1)} %copy.65), calls=%async_computation.1 | async-start | bytes 393216 | tf_op jit(solution)/shard_map/all_to_all | solution.py:150
  48.2 1.3 %copy.56 = bf16[4,256,3,64]{3,0,2,1:T(4,128)(2,1)} copy(bf16[4,256,3,64]{1,3,2,0:T(8,128)(2,1)S(1)} %convolution_bitcast_fusion.1) | data formatting | bytes 786432 | tf_op jit(solution)/shard_map/vmap(hij,jhd->ihd)/transpose | solution.py:37
  49.5 1.4 %select_reduce_fusion = f32[6,3,256]{0,1,2:T(4,128)S(1)} fusion(f32[4,3,256]{0,1,2:T(4,128)S(1)} %copy.53, pred[4,6]{1,0:T(4,128)(4,1)S(1)} %fusion.54), kind=kLoop, calls=%fused_computation.11 | loop fusion | flops 32256 | bytes 30744 | tf_op jit(solution)/shard_map/reduce_max | solution.py:61
  50.9 1.4 %fusion.66 = (f32[2,3,256]{0,1,2:T(4,128)}, f32[2,3,256]{0,1,2:T(4,128)}) fusion(f32[6,3,256]{0,1,2:T(4,128)S(1)} %select_reduce_fusion), kind=kLoop, calls=%fused_computation.118 | loop fusion | bytes 24576 | tf_op jit(solution)/shard_map/slice | solution.py:136
  52.3 1.6 %fusion = f32[3,256,1,6]{3,2,1,0:T(1,128)S(1)} fusion(bf16[4,3,256,1]{0,3,2,1:T(2,128)(2,1)S(1)} %copy.66, f32[6,3,256]{0,1,2:T(4,128)S(1)} %select_reduce_fusion, f32[4,3,256]{0,1,2:T(4,128)S(1)} %copy.53, pred[4,6]{1,0:T(4,128)(4,1)S(1)} %fusion.54), kind=kOutput, calls=%fused_computation.12 | convolution fusion | flops 73728 | bytes 55320 | tf_op jit(solution)/shard_map/pehi,phi->ehi/dot_general | solution.py:63
  54.2 1.4 %fusion.67 = (f32[2,3,256]{0,1,2:T(4,128)}, f32[2,3,256]{0,1,2:T(4,128)}) fusion(f32[6,3,256]{0,1,2:T(4,128)S(1)} %bitcast.71), kind=kLoop, calls=%fused_computation.119 | loop fusion | bytes 24576 | tf_op jit(solution)/shard_map/slice | solution.py:135
  55.5 11.4 %collective-permute-start.6 = (f32[2,3,256]{0,1,2:T(4,128)}, f32[2,3,256]{0,1,2:T(4,128)}, u32[]{:S(2)}, u32[]{:S(2)}) collective-permute-start(f32[2,3,256]{0,1,2:T(4,128)} %get-tuple-element.17), channel_id=1, source_target_pairs={{0,508},{4,0},{8,4},{12,8},{16,12},{20,16},{24,20},{28,24},{32,28}... | collective-permute-start | bytes 18440 | tf_op jit(solution)/shard_map/ppermute | solution.py:29
  66.9 1.9 %collective-permute-start.7 = (f32[2,3,256]{0,1,2:T(4,128)}, f32[2,3,256]{0,1,2:T(4,128)}, u32[]{:S(2)}, u32[]{:S(2)}) collective-permute-start(f32[2,3,256]{0,1,2:T(4,128)} %get-tuple-element.18), channel_id=1, source_target_pairs={{0,4},{4,8},{8,12},{12,16},{16,20},{20,24},{24,28},{28,32},{32,36}... | collective-permute-start | bytes 18440 | tf_op jit(solution)/shard_map/ppermute | solution.py:29
  68.9 1.9 %collective-permute-start.3 = (f32[2,3,256]{0,1,2:T(4,128)}, f32[2,3,256]{0,1,2:T(4,128)S(1)}, u32[]{:S(2)}, u32[]{:S(2)}) collective-permute-start(f32[2,3,256]{0,1,2:T(4,128)} %get-tuple-element.15), channel_id=1, source_target_pairs={{0,4},{4,8},{8,12},{12,16},{16,20},{20,24},{24,28},{28,32},{32,36}... | collective-permute-start | bytes 18440 | tf_op jit(solution)/shard_map/ppermute | solution.py:29
  70.8 2.6 %collective-permute-start.2 = (f32[2,3,256]{0,1,2:T(4,128)}, f32[2,3,256]{0,1,2:T(4,128)}, u32[]{:S(2)}, u32[]{:S(2)}) collective-permute-start(f32[2,3,256]{0,1,2:T(4,128)} %get-tuple-element.16), channel_id=1, source_target_pairs={{0,508},{4,0},{8,4},{12,8},{16,12},{20,16},{24,20},{28,24},{32,28}... | collective-permute-start | bytes 18440 | tf_op jit(solution)/shard_map/ppermute | solution.py:29
  73.4 3.6 %fusion.63 = f32[256,3,64,6]{2,3,1,0:T(8,128)} fusion(bf16[4,256,3,64]{3,0,2,1:T(4,128)(2,1)S(1)} %copy-done.5, f32[6,3,256]{0,1,2:T(4,128)S(1)} %select_reduce_fusion, f32[4,3,256]{0,1,2:T(4,128)S(1)} %copy.53, pred[4,6]{1,0:T(4,128)(4,1)S(1)} %fusion.54), kind=kOutput, calls=%fused_computation.115 | convolution fusion | flops 2396160 | bytes 1603608 | tf_op jit(solution)/shard_map/pehi,pihd->eihd/dot_general | solution.py:64
  77.0 2.3 %copy.57 = f32[256,3,64,6]{0,2,1,3:T(8,128)S(1)} copy(f32[256,3,64,6]{2,3,1,0:T(8,128)} %fusion.63) | data formatting | bytes 2359296 | tf_op jit(solution)/shard_map/pehi,pihd->eihd/dot_general | solution.py:64
  79.3 1.0 fusion.65
  80.3 6.9 %collective-permute-start.4 = (f32[2,256,3,64]{1,3,2,0:T(8,128)}, f32[2,256,3,64]{1,3,2,0:T(8,128)}, u32[]{:S(2)}, u32[]{:S(2)}) collective-permute-start(f32[2,256,3,64]{1,3,2,0:T(8,128)} %get-tuple-element.10), channel_id=1, source_target_pairs={{0,508},{4,0},{8,4},{12,8},{16,12},{20,16},{24,20},{28,24},{32,28}... | collective-permute-start | bytes 1179656 | tf_op jit(solution)/shard_map/ppermute | solution.py:29
  87.2 1.9 %collective-permute-start.5 = (f32[2,256,3,64]{1,3,2,0:T(8,128)}, f32[2,256,3,64]{1,3,2,0:T(8,128)}, u32[]{:S(2)}, u32[]{:S(2)}) collective-permute-start(f32[2,256,3,64]{1,3,2,0:T(8,128)} %get-tuple-element.11), channel_id=1, source_target_pairs={{0,4},{4,8},{8,12},{12,16},{16,20},{20,24},{24,28},{28,32},{32,36}... | collective-permute-start | bytes 1179656 | tf_op jit(solution)/shard_map/ppermute | solution.py:29
  89.2 2.4 %fusion.41 = (f32[2,256,3]{0,2,1:T(4,128)}, f32[2,3,256]{0,1,2:T(4,128)}) fusion(f32[6,3,256]{0,1,2:T(4,128)S(1)} %select_reduce_fusion, f32[2,3,256]{0,1,2:T(4,128)S(1)} %collective-permute-done.3, f32[2,3,256]{0,1,2:T(4,128)} %collective-permute-done.2), kind=kLoop, calls=%fused_computation.79 | loop fusion | flops 4608 | bytes 30720 | tf_op jit(solution)/shard_map/transpose | solution.py:52
  91.6 1.2 copy.54
  92.8 3.4 %fusion.39 = (f32[2,256,3]{0,2,1:T(4,128)}, f32[2,256,3]{0,2,1:T(4,128)}, f32[2,256,3]{0,2,1:T(4,128)}) fusion(f32[2,3,256]{0,1,2:T(4,128)} %collective-permute-done.2, f32[2,3,256]{0,1,2:T(4,128)} %get-tuple-element.7, f32[2,3,256]{0,1,2:T(4,128)} %collective-permute-done.7, f32[2,3,256]{0,1,2:T(4,128)S(1)} %collective-permute-done.3, ...), kind=kLoop, calls=%fused_computation.77 | loop fusion | flops 15360 | bytes 61440 | tf_op jit(solution)/shard_map/transpose | solution.py:52
  96.2 1.2 copy.58
  97.5 1.2 %copy.60 = f32[2,256,3]{1,2,0:T(4,128)S(1)} copy(f32[2,256,3]{0,2,1:T(4,128)} %get-tuple-element.13) | data formatting | bytes 12288 | tf_op jit(solution)/shard_map/transpose | solution.py:54
  98.7 1.2 %copy.59 = f32[2,256,3]{1,2,0:T(4,128)S(1)} copy(f32[2,256,3]{0,2,1:T(4,128)} %get-tuple-element.14) | data formatting | bytes 12288 | tf_op jit(solution)/shard_map/transpose | solution.py:52
  99.9 1.2 %fusion.29 = bf16[2,256,3,64]{1,3,2,0:T(8,128)(2,1)S(1)} fusion(f32[2,256,3,64]{1,3,2,0:T(8,128)} %collective-permute-done.5, f32[2,256,3,64]{1,3,2,0:T(8,128)} %collective-permute-done.4, f32[6,256,3,64]{1,3,2,0:T(8,128)S(1)} %bitcast.74, f32[2,256,3]{1,2,0:T(4,128)S(1)} %copy.60, f32[2,256,3]{1,2,0:T(4,128)S(1)} %copy.59, f32[2,256,3]{1,2,0:T(4,128)S(1)} %copy.58, ...), kind=kLoop, calls=%fused_computation.67 | loop fusion | flops 688128 | bytes 1400832 | tf_op jit(solution)/shard_map/convert_element_type | solution.py:141
  101.5 0.7 copy.62
  102.2 4.5 %all-to-all-start = ((bf16[4,128,192]{1,2,0:T(8,128)(2,1)}), bf16[4,128,192]{1,2,0:T(8,128)(2,1)S(1)}, u32[]{:S(2)}, u32[]{:S(2)}) async-start(bf16[4,128,192]{1,2,0:T(8,128)(2,1)} %copy.62), calls=%async_computation | async-start | bytes 393216 | tf_op jit(solution)/shard_map/all_to_all | solution.py:149
  106.7 1.3 %fusion.9 = f32[128,768]{1,0:T(8,128)S(1)} fusion(bf16[768,768]{1,0:T(8,128)(2,1)} %all-gather.5.cloned.1.call-done, bf16[128,768]{0,1:T(8,128)(2,1)} %bitcast.25), kind=kOutput, calls=%fused_computation.29 | convolution fusion | flops 37945344 | bytes 737280 | tf_op jit(solution)/shard_map/dot_general | solution.py:156
  108.1 1.2 fusion.8
  109.3 1.0 fusion.6
  110.3 1.7 %fusion.4 = bf16[128,768]{1,0:T(8,128)(2,1)} fusion(f32[128,768]{1,0:T(8,128)S(1)} %fusion.6, bf16[768,768]{1,0:T(8,128)(2,1)S(1)} %copy-done.3, bf16[128,768]{0,1:T(8,128)(2,1)} %bitcast.25), kind=kOutput, calls=%fused_computation.21 | convolution fusion | flops 38141952 | bytes 933888 | tf_op jit(solution)/shard_map/dot_general | solution.py:156
  112.1 1.3 %fusion.17 = f32[128,768]{1,0:T(8,128)S(1)} fusion(bf16[768,768]{1,0:T(8,128)(2,1)} %all-gather.3.cloned.1.call-done, bf16[128,768]{0,1:T(8,128)(2,1)S(1)} %bitcast.75), kind=kOutput, calls=%fused_computation.41 | convolution fusion | flops 37945344 | bytes 737280 | tf_op jit(solution)/shard_map/dot_general | solution.py:156
  113.3 1.2 fusion.16
  114.8 0.9 fusion.12
  (63 shorter events, 5.5 us)
Async XLA Ops:
  7.2 1.1 copy-start
  7.2 2.5 %copy-start.6 = (bf16[768,192]{0,1:T(8,128)(2,1)S(1)}, bf16[768,192]{0,1:T(8,128)(2,1)}, u32[]{:S(2)}) copy-start(bf16[768,192]{0,1:T(8,128)(2,1)} %param.14) | copy-start | bytes 884740
  7.2 99.5 %all-gather.5.cloned.1.call-start = ((), (), s32[]{:S(2)}) async-start(), calls=%async_computation.3 | async-start | bytes 1474560 | tf_op jit(solution)/shard_map/all_gather | solution.py:146
  7.9 13.8 %copy-start.2 = (bf16[512,768]{1,0:T(8,128)(2,1)S(1)}, bf16[512,768]{1,0:T(8,128)(2,1)}, u32[]{:S(2)}) copy-start(bf16[512,768]{1,0:T(8,128)(2,1)} %param.12) | copy-start | bytes 2359300
  7.9 104.1 %all-gather.3.cloned.1.call-start = ((), (), s32[]{:S(2)}) async-start(), calls=%async_computation.2 | async-start | bytes 1474560 | tf_op jit(solution)/shard_map/all_gather | solution.py:145
  10.2 16.0 %collective-permute-start.1 = (bf16[2,512,192]{1,2,0:T(8,128)(2,1)S(1)}, bf16[2,512,192]{1,2,0:T(8,128)(2,1)S(1)}, u32[]{:S(2)}, u32[]{:S(2)}) collective-permute-start(bf16[2,512,192]{1,2,0:T(8,128)(2,1)S(1)} %pad_maximum_fusion.1), channel_id=1, source_target_pairs={{4,0},{8,4},{12,8},{16,12},{20,16},{24,20},{28,24},{32,28},{36,32}... | collective-permute-start | bytes 1179656 | tf_op jit(solution)/shard_map/ppermute | solution.py:21
  19.0 9.1 %collective-permute-start = (bf16[2,512,192]{1,2,0:T(8,128)(2,1)S(1)}, bf16[2,512,192]{1,2,0:T(8,128)(2,1)S(1)}, u32[]{:S(2)}, u32[]{:S(2)}) collective-permute-start(bf16[2,512,192]{1,2,0:T(8,128)(2,1)S(1)} %pad_maximum_fusion.1), channel_id=1, source_target_pairs={{0,4},{4,8},{8,12},{12,16},{16,20},{20,24},{24,28},{28,32},{32,36}... | collective-permute-start | bytes 1179656 | tf_op jit(solution)/shard_map/ppermute | solution.py:20
  25.2 0.7 copy-start.7
  25.3 0.7 copy-start.8
  37.3 2.9 %copy-start.1 = (f32[4,3,256,256]{3,2,1,0:T(8,128)S(1)}, f32[4,3,256,256]{3,2,1,0:T(8,128)}, u32[]{:S(2)}) copy-start(f32[4,3,256,256]{3,2,1,0:T(8,128)} %get-tuple-element.26) | copy-start | bytes 9437188
  43.8 58.4 %all-to-all-start.1 = ((bf16[4,128,192]{1,2,0:T(8,128)(2,1)}), bf16[4,128,192]{1,2,0:T(8,128)(2,1)}, u32[]{:S(2)}, u32[]{:S(2)}) async-start(bf16[4,128,192]{1,2,0:T(8,128)(2,1)} %copy.65), calls=%async_computation.1 | async-start | bytes 393216 | tf_op jit(solution)/shard_map/all_to_all | solution.py:150
  53.9 19.5 %copy-start.5 = (bf16[4,256,3,64]{3,0,2,1:T(4,128)(2,1)S(1)}, bf16[4,256,3,64]{3,0,2,1:T(4,128)(2,1)}, u32[]{:S(2)}) copy-start(bf16[4,256,3,64]{3,0,2,1:T(4,128)(2,1)} %copy.56) | copy-start | bytes 1179652
  55.5 37.2 %collective-permute-start.6 = (f32[2,3,256]{0,1,2:T(4,128)}, f32[2,3,256]{0,1,2:T(4,128)}, u32[]{:S(2)}, u32[]{:S(2)}) collective-permute-start(f32[2,3,256]{0,1,2:T(4,128)} %get-tuple-element.17), channel_id=1, source_target_pairs={{0,508},{4,0},{8,4},{12,8},{16,12},{20,16},{24,20},{28,24},{32,28}... | collective-permute-start | bytes 18440 | tf_op jit(solution)/shard_map/ppermute | solution.py:29
  66.9 25.9 %collective-permute-start.7 = (f32[2,3,256]{0,1,2:T(4,128)}, f32[2,3,256]{0,1,2:T(4,128)}, u32[]{:S(2)}, u32[]{:S(2)}) collective-permute-start(f32[2,3,256]{0,1,2:T(4,128)} %get-tuple-element.18), channel_id=1, source_target_pairs={{0,4},{4,8},{8,12},{12,16},{16,20},{20,24},{24,28},{28,32},{32,36}... | collective-permute-start | bytes 18440 | tf_op jit(solution)/shard_map/ppermute | solution.py:29
  68.9 18.4 %collective-permute-start.3 = (f32[2,3,256]{0,1,2:T(4,128)}, f32[2,3,256]{0,1,2:T(4,128)S(1)}, u32[]{:S(2)}, u32[]{:S(2)}) collective-permute-start(f32[2,3,256]{0,1,2:T(4,128)} %get-tuple-element.15), channel_id=1, source_target_pairs={{0,4},{4,8},{8,12},{12,16},{16,20},{20,24},{24,28},{28,32},{32,36}... | collective-permute-start | bytes 18440 | tf_op jit(solution)/shard_map/ppermute | solution.py:29
  70.8 18.4 %collective-permute-start.2 = (f32[2,3,256]{0,1,2:T(4,128)}, f32[2,3,256]{0,1,2:T(4,128)}, u32[]{:S(2)}, u32[]{:S(2)}) collective-permute-start(f32[2,3,256]{0,1,2:T(4,128)} %get-tuple-element.16), channel_id=1, source_target_pairs={{0,508},{4,0},{8,4},{12,8},{16,12},{20,16},{24,20},{28,24},{32,28}... | collective-permute-start | bytes 18440 | tf_op jit(solution)/shard_map/ppermute | solution.py:29
  80.3 19.6 %collective-permute-start.4 = (f32[2,256,3,64]{1,3,2,0:T(8,128)}, f32[2,256,3,64]{1,3,2,0:T(8,128)}, u32[]{:S(2)}, u32[]{:S(2)}) collective-permute-start(f32[2,256,3,64]{1,3,2,0:T(8,128)} %get-tuple-element.10), channel_id=1, source_target_pairs={{0,508},{4,0},{8,4},{12,8},{16,12},{20,16},{24,20},{28,24},{32,28}... | collective-permute-start | bytes 1179656 | tf_op jit(solution)/shard_map/ppermute | solution.py:29
  87.2 12.7 %collective-permute-start.5 = (f32[2,256,3,64]{1,3,2,0:T(8,128)}, f32[2,256,3,64]{1,3,2,0:T(8,128)}, u32[]{:S(2)}, u32[]{:S(2)}) collective-permute-start(f32[2,256,3,64]{1,3,2,0:T(8,128)} %get-tuple-element.11), channel_id=1, source_target_pairs={{0,4},{4,8},{8,12},{12,16},{16,20},{20,24},{24,28},{28,32},{32,36}... | collective-permute-start | bytes 1179656 | tf_op jit(solution)/shard_map/ppermute | solution.py:29
  102.2 9.8 %all-to-all-start = ((bf16[4,128,192]{1,2,0:T(8,128)(2,1)}), bf16[4,128,192]{1,2,0:T(8,128)(2,1)S(1)}, u32[]{:S(2)}, u32[]{:S(2)}) async-start(bf16[4,128,192]{1,2,0:T(8,128)(2,1)} %copy.62), calls=%async_computation | async-start | bytes 393216 | tf_op jit(solution)/shard_map/all_to_all | solution.py:149
  106.7 2.5 %copy-start.3 = (bf16[768,768]{1,0:T(8,128)(2,1)S(1)}, bf16[768,768]{1,0:T(8,128)(2,1)}, u32[]{:S(2)}) copy-start(bf16[768,768]{1,0:T(8,128)(2,1)} %all-gather.5.cloned.1.call-done) | copy-start | bytes 3538948
  112.1 2.5 %copy-start.4 = (bf16[768,768]{1,0:T(8,128)(2,1)S(1)}, bf16[768,768]{1,0:T(8,128)(2,1)}, u32[]{:S(2)}) copy-start(bf16[768,768]{1,0:T(8,128)(2,1)} %all-gather.3.cloned.1.call-done) | copy-start | bytes 3538948
Sparse Core Ops, SparseCore 0:
  10.1 36.3 all-gather.4
  48.6 32.7 all-gather.2
where the time goes:
time: 124 us; the launch traced here: 123 us
  starting transfers between devices  46 us (37%)
  matrix products  24.4 us (20%)
  local copies, waits for them, and re-layouts  23.5 us (19%)
  between operations  15.1 us (12%)
  other arithmetic  10.8 us (9%)
  waiting for transfers between devices  2.64 us (2%)
    ppermute x6, starting transfers between devices, shifted(): return lax.ppermute(value, axis, pairs)  26.7 us
    dot_general x8, matrix products, apply_out(): jnp.dot(rows[:, group * width:(group + 1) * width], weight_full[group * w...  8.89 us
    ppermute x1, starting transfers between devices, with_halo(): after = lax.ppermute(leading, axis, down)  8.79 us
    transpose x2, other arithmetic, combine_three(): a_sum = a_sum + jnp.transpose(scale, (0, 2, 1))[..., None] * a_part  5.83 us
    all_to_all x1, starting transfers between devices, body(): lax.all_to_all(grid_mix, 'head', split_axis=0, concat_axis=1, tiled=True)  4.52 us
    all_to_all x1, starting transfers between devices, body(): lax.all_to_all(obs_mix, 'head', split_axis=0, concat_axis=1, tiled=True)  4.04 us
    another operation x2, local copies, waits for them, and re-layouts, body(): wide_query = widened[0].reshape(3 * blocks, BS, heads_dev, HD)  3.72 us
    transpose x3, local copies, waits for them, and re-layouts, combine_three(): a_sum = a_sum + jnp.transpose(scale, (0, 2, 1))[..., None] * a_part  3.68 us
  transfers between devices with their start and end apart: 12, of which 1 were waited for; matrix products, arithmetic and copies ran while one was open for 44% of the time, Pallas kernels for 0%

commit v1 on v0

v1 whole, which is shorter than its diff:
```python
import jax
import jax.numpy as jnp
from jax import lax
from jax.experimental import pallas as pl
from jax.experimental.pallas import tpu as pltpu
from jax.sharding import PartitionSpec as P

HD = 64
BS = 256
HEADS = 3
WIDTH = HEADS * HD
GROUPS = 4
D = 768
NEG = -1e30
PAY = 3 * BS + 16
NT = (((1,), (1,)), ((), ()))
VMEM_LIMIT = 48 * 1024 * 1024


def dot32(a, b):
    return jnp.dot(a, b, preferred_element_type=jnp.float32)


def lanes(width):
    return lax.broadcasted_iota(jnp.int32, (1, width), 1)


def project_kernel(par, count, seam, grid, obs, w_q, w_gv, w_k, w_ov, pay_a, pay_b):
    slot_b = par[0]
    x = jnp.concatenate(
        [dot32(grid[...], w_q[...]).astype(jnp.bfloat16), dot32(grid[...], w_gv[...]).astype(jnp.bfloat16)], axis=1
    )
    pay_a[: 2 * BS] = x
    pay_b[: 2 * BS] = x
    for pay, slot in ((pay_a, 1 - slot_b), (pay_b, slot_b)):
        rows = obs[pl.ds(pl.multiple_of(slot * BS, BS), BS)]
        pay[2 * BS : 3 * BS] = jnp.concatenate(
            [dot32(rows, w_k[...]).astype(jnp.bfloat16), dot32(rows, w_ov[...]).astype(jnp.bfloat16)], axis=1
        )
        target = (seam[slot] & 1).astype(jnp.float32)
        live = (slot < count[0]).astype(jnp.float32)
        flags = jnp.where(lax.broadcasted_iota(jnp.int32, (16, 2 * WIDTH), 1) < 128, target, live)
        pay[3 * BS :] = flags.astype(jnp.bfloat16)


def side(x, y):
    lane = lanes(BS)
    left = x[:, :BS]
    right = y[:, :BS]
    vals = jnp.where(lane < HD, jnp.bfloat16(1.0), y[:, 2 * HD :])
    out = total = top = None
    for h in range(HEADS):
        pick = jnp.where((lane >= h * HD) & (lane < (h + 1) * HD), 0.125, 0.0).astype(jnp.bfloat16)
        s = lax.dot_general(left * pick, right, NT, preferred_element_type=jnp.float32)
        m = jnp.max(s, axis=1, keepdims=True)
        e = jnp.exp(s - m).astype(jnp.bfloat16)
        o = dot32(e, vals)
        l = o[:, :1]
        if h == 0:
            out, total, top = o, jnp.broadcast_to(l, o.shape), jnp.broadcast_to(m, o.shape)
        else:
            mine = lane >= (h + 1) * HD
            out = jnp.where(mine, o, out)
            total = jnp.where(mine, l, total)
            top = jnp.where(mine, m, top)
    return out, total, top


def merge(first, second):
    top = jnp.maximum(first[2], second[2])
    w1 = jnp.exp(first[2] - top)
    w2 = jnp.exp(second[2] - top)
    return w1 * first[0] + w2 * second[0], w1 * first[1] + w2 * second[1], top


def attend_kernel(par, count, home, seam, pay_a, pay_b, rec_a, rec_b, out, acc, mix):
    slot_b = par[0]
    acc[:, 0] = jnp.zeros_like(acc[:, 0])
    acc[:, 1] = jnp.zeros_like(acc[:, 1])
    acc[:, 2] = jnp.full_like(acc[:, 2], NEG)
    mix[...] = jnp.zeros_like(mix)

    def add(block, part):
        now = merge((acc[block, 0], acc[block, 1], acc[block, 2]), part)
        for i in range(3):
            acc[block, i] = now[i]

    for slot, pay, rec in ((1 - slot_b, pay_a, rec_a), (slot_b, pay_b, rec_b)):

        @pl.when(slot < count[0])
        def _():
            kv = pay[2 * BS : 3 * BS]
            block = home[slot]
            x = pay[pl.ds(pl.multiple_of(block * BS, BS), BS)]
            add(block, side(x, kv))
            x2 = rec[pl.ds(pl.multiple_of((seam[slot] & 1) * BS, BS), BS)]
            o, l, _m = merge(side(kv, x), side(kv, x2))
            mix[2 + slot] = (o / l).astype(jnp.bfloat16)

        flags = rec[3 * BS :, :BS].astype(jnp.float32)
        block_in = jnp.max(flags[:, :128]).astype(jnp.int32)
        live_in = jnp.max(flags[:, 128:]) > 0.5

        @pl.when(live_in)
        def _():
            kv = rec[2 * BS : 3 * BS]
            x = pay[pl.ds(pl.multiple_of(block_in * BS, BS), BS)]
            add(block_in, side(x, kv))

    for block in range(2):
        l = acc[block, 1]
        mix[block] = (acc[block, 0] / jnp.where(l > 0, l, 1.0)).astype(jnp.bfloat16)
    for block in range(2):
        g = mix[block]
        o = mix[2 + block]
        first = jnp.where(lanes(128) < HD, pltpu.roll(o[:, :128], HD, 1), g[:, :128])
        whole = jnp.concatenate([first, g[:, 128:], o[:, 128:]], axis=1)
        out[2 * block] = whole[:128]
        out[2 * block + 1] = whole[128:]


def out_kernel(par, mixes, w_own, w_other, grid_out, obs_out):
    def apply(part, w):
        total = None
        for k in range(GROUPS):
            rows = mixes[k]
            if part == 0:
                rows = rows[:, HD : HD + WIDTH]
            else:
                rows = jnp.concatenate([rows[:, :HD], rows[:, HD + WIDTH :]], axis=1)
            piece = dot32(rows, w[k]).astype(jnp.bfloat16).astype(jnp.float32)
            total = piece if total is None else total + piece
        return total.astype(jnp.bfloat16)

    @pl.when(par[0] == 0)
    def _():
        grid_out[...] = apply(0, w_own)
        obs_out[...] = apply(1, w_other)

    @pl.when(par[0] == 1)
    def _():
        grid_out[...] = apply(0, w_other)
        obs_out[...] = apply(1, w_own)


SMEM = pl.BlockSpec(memory_space=pltpu.SMEM)
VMEM = pl.BlockSpec(memory_space=pltpu.VMEM)
PARAMS = pltpu.CompilerParams(vmem_limit_bytes=VMEM_LIMIT)


def body(
    grid_tokens, obs_tokens, w_query, w_gridval, w_key, w_obsval, w_gridout, w_obsout, obs_count, home_block, seam_block
):
    tiles = lax.axis_size("tile")
    parity = lax.axis_index("tile").astype(jnp.int32) % 2
    par = parity.reshape(1)
    swap_a = [(i, i ^ 1) for i in range(tiles)]
    swap_b = [(i, (i + 1) % tiles if i % 2 else (i - 1) % tiles) for i in range(tiles)]
    pay_shape = jax.ShapeDtypeStruct((PAY, 2 * WIDTH), jnp.bfloat16)
    pay_a, pay_b = pl.pallas_call(
        project_kernel,
        out_shape=(pay_shape, pay_shape),
        in_specs=[SMEM] * 3 + [VMEM] * 6,
        out_specs=(VMEM, VMEM),
        compiler_params=PARAMS,
        cost_estimate=pl.CostEstimate(flops=604_000_000, bytes_accessed=4_000_000, transcendentals=0),
    )(par, obs_count, seam_block, grid_tokens, obs_tokens, w_query, w_gridval, w_key, w_obsval)
    rec_b = lax.ppermute(pay_b, "tile", swap_b)
    rec_a = lax.ppermute(pay_a, "tile", swap_a)
    w_mine = jnp.where(parity == 0, w_gridout, w_obsout)
    w_own = lax.all_to_all(
        jnp.broadcast_to(w_mine[None], (GROUPS,) + w_mine.shape), "head", split_axis=0, concat_axis=0, tiled=True
    )
    w_other = lax.ppermute(w_own, "tile", swap_a)
    mix = pl.pallas_call(
        attend_kernel,
        out_shape=jax.ShapeDtypeStruct((GROUPS, 128, 2 * WIDTH), jnp.bfloat16),
        in_specs=[SMEM] * 4 + [VMEM] * 4,
        out_specs=VMEM,
        scratch_shapes=[pltpu.VMEM((2, 3, BS, BS), jnp.float32), pltpu.VMEM((4, BS, BS), jnp.bfloat16)],
        compiler_params=PARAMS,
        cost_estimate=pl.CostEstimate(flops=1_200_000_000, bytes_accessed=2_400_000, transcendentals=1_600_000),
    )(par, obs_count, home_block, seam_block, pay_a, pay_b, rec_a, rec_b)
    mixes = lax.all_to_all(mix, "head", split_axis=0, concat_axis=0, tiled=True)
    out_shape = jax.ShapeDtypeStruct((128, D), jnp.bfloat16)
    return pl.pallas_call(
        out_kernel,
        out_shape=(out_shape, out_shape),
        in_specs=[SMEM] + [VMEM] * 3,
        out_specs=(VMEM, VMEM),
        compiler_params=PARAMS,
        cost_estimate=pl.CostEstimate(flops=302_000_000, bytes_accessed=3_000_000, transcendentals=0),
    )(par, mixes, w_own, w_other)


def solution(mesh):
    return jax.shard_map(
        body,
        mesh=mesh,
        in_specs=(
            P("tile", None),
            P("tile", None),
            P(None, "head"),
            P(None, "head"),
            P(None, "head"),
            P(None, "head"),
            P("head", None),
            P("head", None),
            P("tile"),
            P("tile"),
            P("tile"),
        ),
        out_specs=(P(("tile", "head"), None), P(("tile", "head"), None)),
        check_vma=False,
    )
```

time: 124 us -> 72.4 us (0.58)
  the two profiles are of different devices: /device:TPU:1 before, /device:TPU:2 now
where the time goes in v1:
time: 72.4 us; the launch traced here: 72 us
  blocking collectives  29.6 us (41%)
  starting transfers between devices  17.9 us (25%)
  Pallas kernels  11.5 us (16%)
  waiting for transfers between devices  7.68 us (11%)
  local copies, waits for them, and re-layouts  2.88 us (4%)
  between operations  1.45 us (2%)
  other arithmetic  1 us (1%)
    all_to_all x1, blocking collectives, body(): lax.all_to_all(jnp.broadcast_to(w_mine[None], (GROUPS,) + w_mine.shape),...  19.8 us
    ppermute x1, starting transfers between devices, body(): rec_b = lax.ppermute(pay_b, 'tile', swap_b)  13.5 us
    all_to_all x1, blocking collectives, body(): mixes = lax.all_to_all(mix, 'head', split_axis=0, concat_axis=0, tiled=True)  9.77 us
    ppermute x1, waiting for transfers between devices, body(): rec_b = lax.ppermute(pay_b, 'tile', swap_b)  7.67 us
    pallas_call x1, Pallas kernels, body(): pl.pallas_call(attend_kernel, out_shape=jax.ShapeDtypeStruct((GROUPS, 128...  7.21 us
    unnamed x18, local copies, waits for them, and re-layouts  2.8 us
    pallas_call x1, Pallas kernels, body(): pl.pallas_call(out_kernel, out_shape=(out_shape, out_shape), in_specs=[SM...  2.66 us
    ppermute x1, starting transfers between devices, body(): rec_a = lax.ppermute(pay_a, 'tile', swap_a)  2.41 us
  transfers between devices with their start and end apart: 3, of which 1 were waited for; matrix products, arithmetic and copies ran while one was open for 2% of the time, Pallas kernels for 12%

profile of v1, /device:TPU:2, one launch (start us, length us, event | category | flops | bytes accessed | tf_op | source)
XLA Modules:
  0.0 72.0 jit_solution(9933514056104113600)
XLA Ops:
  0.6 1.0 %broadcast_select_fusion = bf16[192,768]{1,0:T(8,128)(2,1)S(1)} fusion(bf16[192,768]{1,0:T(8,128)(2,1)} %param.17, bf16[192,768]{1,0:T(8,128)(2,1)} %param.18, pred[]{:T(512)S(6)} %eq.5), kind=kLoop, calls=%fused_computation | loop fusion | flops 147456 | bytes 884737 | tf_op jit(solution)/shard_map/jit(_where)/select_n | solution.py:170
  1.6 0.1 broadcast_in_dim.2
  1.7 0.0 copy-start.4
  1.7 0.0 copy-start.5
  1.8 19.8 %all_to_all.10.w_own = bf16[4,192,768]{2,1,0:T(8,128)(2,1)S(1)} all-to-all(bf16[4,192,768]{2,1,0:T(8,128)(2,1)S(1)} %broadcast_in_dim.2), channel_id=1, replica_groups=mesh['tile'=128,'head'=4] {'head'}, dimensions={0} | all-to-all | bytes 2359296 | tf_op jit(solution)/shard_map/all_to_all | solution.py:171
  21.6 0.0 copy-start.6
  21.6 2.0 %collective-permute-start.2 = (bf16[4,192,768]{2,1,0:T(8,128)(2,1)S(1)}, bf16[4,192,768]{2,1,0:T(8,128)(2,1)}, u32[]{:S(2)}, u32[]{:S(2)}) collective-permute-start(bf16[4,192,768]{2,1,0:T(8,128)(2,1)S(1)} %all_to_all.10.w_own), channel_id=1, source_target_pairs={{0,4},{4,0},{8,12},{12,8},{16,20},{20,16},{24,28},{28,24},{32,36},... | collective-permute-start | bytes 3538952 | tf_op jit(solution)/shard_map/ppermute | solution.py:174
  24.3 0.0 copy-done.4
  24.3 0.2 copy.13.w_q
  24.4 0.0 copy-done.5
  24.5 0.0 copy-start
  24.5 0.0 copy-start.2
  24.5 0.2 copy.14.w_gv
  24.7 0.0 copy-done.6
  24.7 0.2 copy.15.w_k
  24.8 1.1 %copy.16.w_ov = bf16[768,192]{1,0:T(8,128)(2,1)S(1)} copy(bf16[768,192]{0,1:T(8,128)(2,1)} %param.16) | data formatting | bytes 589824 | tf_op args[5]
  26.0 0.0 copy-done
  26.0 0.0 copy-done.2
  26.0 0.0 copy-start.1
  26.0 1.1 %copy-done.1 = bf16[512,768]{1,0:T(8,128)(2,1)S(1)} copy-done((bf16[512,768]{1,0:T(8,128)(2,1)S(1)}, bf16[512,768]{1,0:T(8,128)(2,1)}, u32[]{:S(2)}) %copy-start.1) | copy-done | bytes 786456
  27.1 0.0 copy-start.3
  27.1 1.6 %shard_map.122 = (bf16[784,384]{1,0:T(8,128)(2,1)S(1)}, bf16[784,384]{1,0:T(8,128)(2,1)S(1)}) custom-call(s32[1]{0:T(128)} %bitcast.par, s32[1]{0:T(128)S(6)} %copy.17.count, s32[2]{0:T(128)S(1)} %copy-done.2, bf16[512,768]{1,0:T(8,128)(2,1)S(1)} %copy-done, bf16[512,768]{1,0:T(8,128)(2,1)S(1)} %copy-done.1, bf16[768,192]{1,0:T(8,128)(2,1)S(1)} %copy.13.w_q, ...), custom_call_target="tpu_custom_call" | custom-call | flops 604000000 | bytes 4000000 | tf_op jit(solution)/shard_map/pallas_call | solution.py:160
  28.7 2.4 %collective-permute-start = (bf16[784,384]{1,0:T(8,128)(2,1)S(1)}, bf16[784,384]{1,0:T(8,128)(2,1)S(1)}, u32[]{:S(2)}, u32[]{:S(2)}) collective-permute-start(bf16[784,384]{1,0:T(8,128)(2,1)S(1)} %get-tuple-element.4.pay_a), channel_id=1, source_target_pairs={{0,4},{4,0},{8,12},{12,8},{16,20},{20,16},{24,28},{28,24},{32,36},... | collective-permute-start | bytes 1806344 | tf_op jit(solution)/shard_map/ppermute | solution.py:169
  31.1 13.5 %collective-permute-start.1 = (bf16[784,384]{1,0:T(8,128)(2,1)S(1)}, bf16[784,384]{1,0:T(8,128)(2,1)S(1)}, u32[]{:S(2)}, u32[]{:S(2)}) collective-permute-start(bf16[784,384]{1,0:T(8,128)(2,1)S(1)} %get-tuple-element.5.pay_b), channel_id=1, source_target_pairs={{0,508},{4,8},{8,4},{12,16},{16,12},{20,24},{24,20},{28,32},{32,28... | collective-permute-start | bytes 1806344 | tf_op jit(solution)/shard_map/ppermute | solution.py:168
  44.6 0.0 collective-permute-done.rec_a
  44.6 7.7 %collective-permute-done.1.rec_b = bf16[784,384]{1,0:T(8,128)(2,1)S(1)} collective-permute-done((bf16[784,384]{1,0:T(8,128)(2,1)S(1)}, bf16[784,384]{1,0:T(8,128)(2,1)S(1)}, u32[]{:S(2)}, u32[]{:S(2)}) %collective-permute-start.1) | collective-permute-done | bytes 602144 | tf_op jit(solution)/shard_map/ppermute | solution.py:168
  52.3 0.0 copy-done.3
  52.3 7.2 %shard_map.123 = bf16[4,128,384]{2,1,0:T(8,128)(2,1)S(1)} custom-call(s32[1]{0:T(128)} %bitcast.par, s32[1]{0:T(128)S(6)} %copy.17.count, s32[2]{0:T(128)S(1)} %copy-done.3, s32[2]{0:T(128)S(1)} %copy-done.2, bf16[784,384]{1,0:T(8,128)(2,1)S(1)} %get-tuple-element.4.pay_a, bf16[784,384]{1,0:T(8,128)(2,1)S(1)} %get-tuple-element.5.pay_b, ...), custom_call_target="tpu_custom_call" | custom-call | flops 1200000000 | bytes 2400000 | tf_op jit(solution)/shard_map/pallas_call | solution.py:175
  59.5 9.8 %all_to_all.11.mixes = bf16[4,128,384]{2,1,0:T(8,128)(2,1)S(1)} all-to-all(bf16[4,128,384]{2,1,0:T(8,128)(2,1)S(1)} %shard_map.123), channel_id=1, replica_groups=mesh['tile'=128,'head'=4] {'head'}, dimensions={0} | all-to-all | bytes 786432 | tf_op jit(solution)/shard_map/all_to_all | solution.py:184
  69.3 0.0 collective-permute-done.2.w_other
  69.3 2.7 %shard_map.124 = (bf16[128,768]{1,0:T(8,128)(2,1)}, bf16[128,768]{1,0:T(8,128)(2,1)}) custom-call(s32[1]{0:T(128)} %bitcast.par, bf16[4,128,384]{2,1,0:T(8,128)(2,1)S(1)} %all_to_all.11.mixes, bf16[4,192,768]{2,1,0:T(8,128)(2,1)S(1)} %all_to_all.10.w_own, bf16[4,192,768]{2,1,0:T(8,128)(2,1)} %collective-permute-done.2.w_other), custom_call_target="tpu_custom_call" | custom-call | flops 302000000 | bytes 3000000 | tf_op jit(solution)/shard_map/pallas_call | solution.py:186
Async XLA Ops:
  1.7 22.5 %copy-start.4 = (bf16[768,192]{0,1:T(8,128)(2,1)S(1)}, bf16[768,192]{0,1:T(8,128)(2,1)}, u32[]{:S(2)}) copy-start(bf16[768,192]{0,1:T(8,128)(2,1)} %param.13) | copy-start | bytes 884740
  1.7 22.7 %copy-start.5 = (bf16[768,192]{0,1:T(8,128)(2,1)S(1)}, bf16[768,192]{0,1:T(8,128)(2,1)}, u32[]{:S(2)}) copy-start(bf16[768,192]{0,1:T(8,128)(2,1)} %param.14) | copy-start | bytes 884740
  21.6 3.1 %copy-start.6 = (bf16[768,192]{0,1:T(8,128)(2,1)S(1)}, bf16[768,192]{0,1:T(8,128)(2,1)}, u32[]{:S(2)}) copy-start(bf16[768,192]{0,1:T(8,128)(2,1)} %param.15) | copy-start | bytes 884740
  21.6 47.7 %collective-permute-start.2 = (bf16[4,192,768]{2,1,0:T(8,128)(2,1)S(1)}, bf16[4,192,768]{2,1,0:T(8,128)(2,1)}, u32[]{:S(2)}, u32[]{:S(2)}) collective-permute-start(bf16[4,192,768]{2,1,0:T(8,128)(2,1)S(1)} %all_to_all.10.w_own), channel_id=1, source_target_pairs={{0,4},{4,0},{8,12},{12,8},{16,20},{20,16},{24,28},{28,24},{32,36},... | collective-permute-start | bytes 3538952 | tf_op jit(solution)/shard_map/ppermute | solution.py:174
  24.5 1.5 %copy-start = (bf16[512,768]{1,0:T(8,128)(2,1)S(1)}, bf16[512,768]{1,0:T(8,128)(2,1)}, u32[]{:S(2)}) copy-start(bf16[512,768]{1,0:T(8,128)(2,1)} %grid.1) | copy-start | bytes 2359300
  24.5 1.5 %copy-start.2 = (s32[2]{0:T(128)S(1)}, s32[2]{0:T(128)}, u32[]{:S(2)}) copy-start(s32[2]{0:T(128)} %seam.3) | copy-start | bytes 28
  26.0 1.1 %copy-start.1 = (bf16[512,768]{1,0:T(8,128)(2,1)S(1)}, bf16[512,768]{1,0:T(8,128)(2,1)}, u32[]{:S(2)}) copy-start(bf16[512,768]{1,0:T(8,128)(2,1)} %obs.1) | copy-start | bytes 2359300
  27.1 25.2 %copy-start.3 = (s32[2]{0:T(128)S(1)}, s32[2]{0:T(128)}, u32[]{:S(2)}) copy-start(s32[2]{0:T(128)} %home.1) | copy-start | bytes 28
  28.7 15.9 %collective-permute-start = (bf16[784,384]{1,0:T(8,128)(2,1)S(1)}, bf16[784,384]{1,0:T(8,128)(2,1)S(1)}, u32[]{:S(2)}, u32[]{:S(2)}) collective-permute-start(bf16[784,384]{1,0:T(8,128)(2,1)S(1)} %get-tuple-element.4.pay_a), channel_id=1, source_target_pairs={{0,4},{4,0},{8,12},{12,8},{16,20},{20,16},{24,28},{28,24},{32,36},... | collective-permute-start | bytes 1806344 | tf_op jit(solution)/shard_map/ppermute | solution.py:169
  31.1 21.2 %collective-permute-start.1 = (bf16[784,384]{1,0:T(8,128)(2,1)S(1)}, bf16[784,384]{1,0:T(8,128)(2,1)S(1)}, u32[]{:S(2)}, u32[]{:S(2)}) collective-permute-start(bf16[784,384]{1,0:T(8,128)(2,1)S(1)} %get-tuple-element.5.pay_b), channel_id=1, source_target_pairs={{0,508},{4,8},{8,4},{12,16},{16,12},{20,24},{24,20},{28,32},{32,28... | collective-permute-start | bytes 1806344 | tf_op jit(solution)/shard_map/ppermute | solution.py:168

commit v2 on v1

v2 whole, which is shorter than its diff:
```python
import jax
import jax.numpy as jnp
from jax import lax
from jax.experimental import pallas as pl
from jax.experimental.pallas import tpu as pltpu
from jax.sharding import PartitionSpec as P

HD = 64
BS = 256
HEADS = 3
WIDTH = HEADS * HD
PAIR = 2 * WIDTH
GROUPS = 4
D = 768
NEG = -1e30
ROWS_O = HD + 16
PAY = 3 * PAIR + 16
NT = (((1,), (1,)), ((), ()))
TN = (((0,), (0,)), ((), ()))
VMEM_LIMIT = 48 * 1024 * 1024


def dot32(a, b):
    return jnp.dot(a, b, preferred_element_type=jnp.float32)


def parity():
    return lax.axis_index("tile") % 2


def slots():
    return 1 - parity(), parity()


def write_flags(pay, slot, count, seam):
    target = (seam[slot] & 1).astype(jnp.float32)
    live = (slot < count[0]).astype(jnp.float32)
    flags = jnp.where(lax.broadcasted_iota(jnp.int32, (16, BS), 1) < 128, target, live)
    pay[3 * PAIR :] = flags.astype(jnp.bfloat16)


def project_kernel(
    count, seam_hbm, grid, obs, w_q, w_gv, w_k, w_ov, w_g, w_o, pay_a, pay_b, spread, tok, wts, seam, sems, sem_w
):
    slot_a, slot_b = slots()

    def rows(ref, block):
        return ref.at[pl.ds(pl.multiple_of(block * BS, BS), BS)]

    weights = (w_q, w_gv, w_k, w_ov)
    load_w = [pltpu.make_async_copy(w, wts.at[pl.ds(i * WIDTH, WIDTH)], sems.at[i]) for i, w in enumerate(weights)]
    load_g = pltpu.make_async_copy(grid, tok.at[pl.ds(0, 2 * BS)], sems.at[4])
    load_b = pltpu.make_async_copy(rows(obs, slot_b), tok.at[pl.ds(2 * BS, BS)], sems.at[5])
    load_a = pltpu.make_async_copy(rows(obs, slot_a), tok.at[pl.ds(3 * BS, BS)], sems.at[6])
    load_seam = pltpu.make_async_copy(seam_hbm, seam, sems.at[7])
    for copy in (load_w[0], load_w[1], load_g, load_w[2], load_w[3], load_b, load_a, load_seam):
        copy.start()

    def send(ref, start):
        for k in range(GROUPS):
            copy = pltpu.make_async_copy(ref, spread.at[k], sem_w.at[k])
            copy.start() if start else copy.wait()

    @pl.when(slot_b == 0)
    def _():
        send(w_g, True)

    @pl.when(slot_b == 1)
    def _():
        send(w_o, True)

    def project(i):
        w = wts[i * PAIR : (i + 1) * PAIR]
        t = tok[2 * i * BS : 2 * (i + 1) * BS]
        return lax.dot_general(w, t, NT, preferred_element_type=jnp.float32).astype(jnp.bfloat16)

    load_w[0].wait()
    load_w[1].wait()
    load_g.wait()
    x = project(0)
    for block in range(2):
        part = x[:, block * BS : (block + 1) * BS]
        pay_a[block * PAIR : (block + 1) * PAIR] = part
        pay_b[block * PAIR : (block + 1) * PAIR] = part
    load_w[2].wait()
    load_w[3].wait()
    load_b.wait()
    load_a.wait()
    x = project(1)
    pay_b[2 * PAIR : 3 * PAIR] = x[:, :BS]
    pay_a[2 * PAIR : 3 * PAIR] = x[:, BS:]
    load_seam.wait()
    write_flags(pay_a, slot_a, count, seam)
    write_flags(pay_b, slot_b, count, seam)
    send(w_g, False)


def row_major(x_t):
    return jnp.transpose(x_t) * jnp.bfloat16(0.125)


def side(left, right_t, vals_t):
    lane = lax.broadcasted_iota(jnp.int32, (1, WIDTH), 1)
    ones = jnp.ones((ROWS_O - HD, BS), jnp.bfloat16)
    parts = []
    for h in range(HEADS):
        mine = (lane >= h * HD) & (lane < (h + 1) * HD)
        s = dot32(jnp.where(mine, left, jnp.bfloat16(0.0)), right_t)
        m = jnp.max(s, axis=0, keepdims=True)
        e = jnp.exp(s - m).astype(jnp.bfloat16)
        parts.append((dot32(jnp.concatenate([vals_t[h * HD : (h + 1) * HD], ones], axis=0), e), m))
    return parts


def fold(acc, top, index, parts):
    for h, (o, m) in enumerate(parts):
        old = top[index, h, :1]
        new = jnp.maximum(old, m)
        acc[index, h] = acc[index, h] * jnp.exp(old - new) + o * jnp.exp(m - new)
        top[index, h] = jnp.broadcast_to(new, (8, BS))


def put(acc, top, index, parts):
    for h, (o, m) in enumerate(parts):
        acc[index, h] = o
        top[index, h] = jnp.broadcast_to(m, (8, BS))


def block_rows(ref, block):
    start = pl.multiple_of(block * PAIR, WIDTH)
    return ref[pl.ds(start, WIDTH)], ref[pl.ds(pl.multiple_of(start + WIDTH, WIDTH), WIDTH)]


def home_kernel(count, home, pay_a, pay_b, acc, top):
    acc[...] = jnp.zeros_like(acc)
    top[...] = jnp.full_like(top, NEG)
    for i, (slot, pay) in enumerate(zip(slots(), (pay_a, pay_b))):

        @pl.when(slot < count[0])
        def _():
            block = home[slot]
            q_t, gv_t = block_rows(pay, block)
            k_t, ov_t = block_rows(pay, 2)
            fold(acc, top, block, side(row_major(k_t), q_t, ov_t))
            put(acc, top, 2 + i, side(row_major(q_t), k_t, gv_t))


def seam_step(i, count, seam, pay, rec, acc, top):
    slot = slots()[i]
    flags = rec[3 * PAIR :].astype(jnp.float32)
    block_in = jnp.max(flags[:, :128]).astype(jnp.int32)
    live_in = jnp.max(flags[:, 128:]) > 0.5

    @pl.when(live_in)
    def _():
        q_t, _gv = block_rows(pay, block_in)
        k_t, ov_t = block_rows(rec, 2)
        fold(acc, top, block_in, side(row_major(k_t), q_t, ov_t))

    @pl.when(slot < count[0])
    def _():
        q_t, gv_t = block_rows(rec, seam[slot] & 1)
        k_t, _ov = block_rows(pay, 2)
        fold(acc, top, 2 + i, side(row_major(q_t), k_t, gv_t))


def near_kernel(count, seam, pay, rec, _acc, _top, acc, top):
    seam_step(0, count, seam, pay, rec, acc, top)


def far_kernel(count, seam, pay, rec, _acc, _top, *refs):
    outs, (acc, top, mix) = refs[:-3], refs[-3:]
    seam_step(1, count, seam, pay, rec, acc, top)
    if len(outs) == 1:
        mix = outs[0]
    slot_a, slot_b = slots()
    for index in range(4):
        if index < 2:
            chunk, first = 2 * index, 0
        else:
            chunk, first = 2 * (slot_a if index == 2 else slot_b), WIDTH
        for h in range(HEADS):
            o = acc[index, h]
            l = o[HD : HD + 1]
            value = (o[:HD] / jnp.where(l > 0, l, 1.0)).astype(jnp.bfloat16)
            at = first + h * HD
            mix[chunk, at : at + HD] = value[:, :128]
            mix[chunk + 1, at : at + HD] = value[:, 128:]
    if len(outs) > 1:
        for s, out in enumerate(outs):
            out[...] = mix[(lax.axis_index("head") + s) % GROUPS]


def out_kernel(*refs):
    mixes, (w_own, w_other, grid_out, obs_out) = refs[:-4], refs[-4:]

    def apply(part, w):
        total = None
        for s in range(GROUPS):
            if len(mixes) == 1:
                k, mix = s, mixes[0].at[s]
            else:
                k, mix = (lax.axis_index("head") + GROUPS - s) % GROUPS, mixes[s]
            rows = mix[part * WIDTH : (part + 1) * WIDTH]
            piece = lax.dot_general(rows, w[k], TN, preferred_element_type=jnp.float32)
            piece = piece.astype(jnp.bfloat16).astype(jnp.float32)
            total = piece if total is None else total + piece
        return total.astype(jnp.bfloat16)

    @pl.when(parity() == 0)
    def _():
        grid_out[...] = apply(0, w_own)
        obs_out[...] = apply(1, w_other)

    @pl.when(parity() == 1)
    def _():
        grid_out[...] = apply(0, w_other)
        obs_out[...] = apply(1, w_own)


SMEM = pl.BlockSpec(memory_space=pltpu.SMEM)
VMEM = pl.BlockSpec(memory_space=pltpu.VMEM)
ANY = pl.BlockSpec(memory_space=pltpu.HBM)
PARAMS = pltpu.CompilerParams(vmem_limit_bytes=VMEM_LIMIT)


def in_hbm(x):
    return pltpu.with_memory_space_constraint(x, pltpu.HBM)


def in_vmem(x):
    return pltpu.with_memory_space_constraint(x, pltpu.VMEM)


def cost(flops, moved, exps=0):
    return pl.CostEstimate(flops=flops, bytes_accessed=moved, transcendentals=exps)


MIX_BY_PERMUTE = False


def body(
    grid_tokens, obs_tokens, w_query, w_gridval, w_key, w_obsval, w_gridout, w_obsout, obs_count, home_block, seam_block
):
    tiles = lax.axis_size("tile")
    swap_a = [(i, i ^ 1) for i in range(tiles)]
    swap_b = [(i, (i + 1) % tiles if i % 2 else (i - 1) % tiles) for i in range(tiles)]
    f32, bf16 = jnp.float32, jnp.bfloat16
    pay_shape = pltpu.VMEM((PAY, BS), bf16)
    acc_shape = pltpu.VMEM((4, HEADS, ROWS_O, BS), f32)
    top_shape = pltpu.VMEM((4, HEADS, 8, BS), f32)
    mix_shape = jax.ShapeDtypeStruct((PAIR, 128), bf16)
    mixes_shape = pltpu.VMEM((GROUPS, PAIR, 128), bf16)
    w_shape = pltpu.VMEM((GROUPS, WIDTH, D), bf16)
    out_shape = jax.ShapeDtypeStruct((128, D), bf16)

    pay_a, pay_b, w_spread = pl.pallas_call(
        project_kernel,
        out_shape=(pay_shape, pay_shape, w_shape),
        in_specs=[SMEM] + [ANY] * 9,
        out_specs=(VMEM, VMEM, VMEM),
        scratch_shapes=[
            pltpu.VMEM((4 * BS, D), bf16),
            pltpu.VMEM((4 * WIDTH, D), bf16),
            pltpu.SMEM((2,), jnp.int32),
            pltpu.SemaphoreType.DMA((8,)),
            pltpu.SemaphoreType.DMA((GROUPS,)),
        ],
        compiler_params=PARAMS,
        cost_estimate=cost(1, 1),
    )(
        obs_count,
        *map(
            in_hbm,
            (seam_block, grid_tokens, obs_tokens, w_query.T, w_gridval.T, w_key.T, w_obsval.T, w_gridout, w_obsout),
        ),
    )
    w_own = lax.all_to_all(w_spread, "head", split_axis=0, concat_axis=0, tiled=True)
    rec_b = lax.ppermute(pay_b, "tile", swap_b)
    acc, top = pl.pallas_call(
        home_kernel,
        out_shape=(acc_shape, top_shape),
        in_specs=[SMEM] * 2 + [VMEM] * 2,
        out_specs=(VMEM, VMEM),
        compiler_params=PARAMS,
        cost_estimate=cost(10**10, 1),
    )(obs_count, home_block, pay_a, pay_b)
    pay_a2 = pay_a
    rec_a = lax.ppermute(pay_a2, "tile", swap_a)
    acc, top = pl.pallas_call(
        near_kernel,
        out_shape=(acc_shape, top_shape),
        in_specs=[SMEM] * 2 + [VMEM] * 4,
        out_specs=(VMEM, VMEM),
        input_output_aliases={4: 0, 5: 1},
        compiler_params=PARAMS,
        cost_estimate=cost(1, 1),
    )(obs_count, seam_block, pay_a, in_vmem(rec_a), acc, top)
    count = GROUPS if MIX_BY_PERMUTE else 1
    mixes = pl.pallas_call(
        far_kernel,
        out_shape=((mix_shape,) * GROUPS if MIX_BY_PERMUTE else (mixes_shape,)) + (acc_shape, top_shape),
        in_specs=[SMEM] * 2 + [VMEM] * 4,
        out_specs=(VMEM,) * (count + 2),
        input_output_aliases={4: count, 5: count + 1},
        scratch_shapes=[pltpu.VMEM(mixes_shape.shape if MIX_BY_PERMUTE else (1, 16, 128), bf16)],
        compiler_params=PARAMS,
        cost_estimate=cost(1, 1),
    )(obs_count, seam_block, pay_b, in_vmem(rec_b), acc, top)
    late = mixes[0]
    if MIX_BY_PERMUTE:
        mixes = [mixes[0]] + [
            lax.ppermute(mixes[s], "head", [(i, (i + s) % GROUPS) for i in range(GROUPS)]) for s in (1, 2, 3)
        ]
    else:
        mixes = [lax.all_to_all(mixes[0], "head", split_axis=0, concat_axis=0, tiled=True)]
    w_own2, _ = lax.optimization_barrier((w_own, rec_a))
    w_other = lax.ppermute(w_own2, "tile", swap_a)
    return pl.pallas_call(
        out_kernel,
        out_shape=(out_shape, out_shape),
        in_specs=[VMEM] * (count + 2),
        out_specs=(VMEM, VMEM),
        compiler_params=PARAMS,
        cost_estimate=cost(1, 1),
    )(*map(in_vmem, mixes), in_vmem(w_own), in_vmem(w_other))


def solution(mesh):
    return jax.shard_map(
        body,
        mesh=mesh,
        in_specs=(
            P("tile", None),
            P("tile", None),
            P(None, "head"),
            P(None, "head"),
            P(None, "head"),
            P(None, "head"),
            P("head", None),
            P("head", None),
            P("tile"),
            P("tile"),
            P("tile"),
        ),
        out_specs=(P(("tile", "head"), None), P(("tile", "head"), None)),
        check_vma=False,
    )
```

time: 72.4 us -> 50.5 us (0.70)
  blocking collectives: 29.6 us -> 10.5 us
  waiting for transfers between devices: 7.68 us -> 0.01 us
  starting transfers between devices: 17.9 us -> 22.7 us
  Pallas kernels: 11.5 us -> 14.7 us
  local copies, waits for them, and re-layouts: 2.88 us -> 0.83 us
  other arithmetic: 1 us -> 0 us
    all_to_all x2 -> x1, blocking collectives: 29.6 us -> 10.5 us  [body(): lax.all_to_all(mixes[0], 'head', split_axis=0, concat_axis=0, tiled=True)]
    all_to_all x0 -> x1, starting transfers between devices: none -> 9.42 us  [body(): lax.all_to_all(w_spread, 'head', split_axis=0, concat_axis=0, tiled=True)]
    ppermute x1, waiting for transfers between devices: 7.67 us -> 0.01 us  [body(): rec_b = lax.ppermute(pay_b, 'tile', swap_b)]
    ppermute x1, starting transfers between devices: 13.5 us -> 9.38 us  [body(): rec_b = lax.ppermute(pay_b, 'tile', swap_b)]
    pallas_call x3 -> x5, Pallas kernels: 11.5 us -> 14.7 us  [the longest x1 4.16 us: body(): pl.pallas_call(home_kernel, out_shape=(acc_shape, top_shape), in_specs=[S...]
    unnamed x18 -> x8, local copies, waits for them, and re-layouts: 2.8 us -> 0.83 us
    select_n x1 -> x0, other arithmetic: 1 us -> none  [body(): w_mine = jnp.where(parity == 0, w_gridout, w_obsout)]
  transfers between devices with their start and end apart: 3 -> 4, of which waited for: 1 -> 0; matrix products, arithmetic and copies ran while one was open for 2% -> 0% of each run, Pallas kernels for 12% -> 19%
where the time goes in v2:
time: 50.5 us; the launch traced here: 50.2 us
  starting transfers between devices  22.7 us (45%)
  Pallas kernels  14.7 us (29%)
  blocking collectives  10.5 us (21%)
  between operations  1.4 us (3%)
  local copies, waits for them, and re-layouts  0.83 us (2%)
    all_to_all x1, blocking collectives, body(): lax.all_to_all(mixes[0], 'head', split_axis=0, concat_axis=0, tiled=True)  10.5 us
    all_to_all x1, starting transfers between devices, body(): lax.all_to_all(w_spread, 'head', split_axis=0, concat_axis=0, tiled=True)  9.42 us
    ppermute x1, starting transfers between devices, body(): rec_b = lax.ppermute(pay_b, 'tile', swap_b)  9.38 us
    pallas_call x1, Pallas kernels, body(): pl.pallas_call(home_kernel, out_shape=(acc_shape, top_shape), in_specs=[S...  4.16 us
    pallas_call x1, Pallas kernels, body(): pl.pallas_call(project_kernel, out_shape=(pay_shape, pay_shape, w_shape),...  3.93 us
    pallas_call x1, Pallas kernels, body(): pl.pallas_call(far_kernel, out_shape=((mix_shape,) * GROUPS if MIX_BY_PER...  2.63 us
    pallas_call x1, Pallas kernels, body(): pl.pallas_call(near_kernel, out_shape=(acc_shape, top_shape), in_specs=[S...  2.57 us
    ppermute x1, starting transfers between devices, body(): w_other = lax.ppermute(w_own2, 'tile', swap_a)  2.04 us
  transfers between devices with their start and end apart: 4, of which 0 were waited for; matrix products, arithmetic and copies ran while one was open for 0% of the time, Pallas kernels for 19%

profile of v2, /device:TPU:2, one launch (start us, length us, event | category | flops | bytes accessed | tf_op | source)
XLA Modules:
  0.0 50.2 jit_solution(3511554358463583986)
XLA Ops:
  1.3 3.9 %shard_map.122 = (bf16[1168,256]{1,0:T(8,128)(2,1)S(1)}, bf16[1168,256]{1,0:T(8,128)(2,1)S(1)}, bf16[4,192,768]{2,1,0:T(8,128)(2,1)}) custom-call(s32[1]{0:T(128)S(6)} %copy.21.count, s32[2]{0:T(128)} %seam.3, bf16[512,768]{1,0:T(8,128)(2,1)} %grid.1, bf16[512,768]{1,0:T(8,128)(2,1)} %obs.1, bf16[192,768]{1,0:T(8,128)(2,1)} %bitcast.4, ...), custom_call_target="tpu_custom_call" | custom-call | flops 1 | bytes 1 | tf_op jit(solution)/shard_map/pallas_call | solution.py:257
  5.2 0.0 copy-start.3
  5.2 9.4 %all-to-all-start.1 = ((bf16[4,192,768]{2,1,0:T(8,128)(2,1)}), bf16[4,192,768]{2,1,0:T(8,128)(2,1)S(1)}, u32[]{:S(2)}, u32[]{:S(2)}) async-start(bf16[4,192,768]{2,1,0:T(8,128)(2,1)} %get-tuple-element.18), calls=%async_computation.1 | async-start | bytes 2359296 | tf_op jit(solution)/shard_map/all_to_all | solution.py:278
  14.6 1.9 %collective-permute-start.1 = (bf16[1168,256]{1,0:T(8,128)(2,1)S(1)}, bf16[1168,256]{1,0:T(8,128)(2,1)S(1)}, u32[]{:S(2)}, u32[]{:S(2)}) collective-permute-start(bf16[1168,256]{1,0:T(8,128)(2,1)S(1)} %get-tuple-element.12.pay_a.pay), channel_id=1, source_target_pairs={{0,4},{4,0},{8,12},{12,8},{16,20},{20,16},{24,28},{28,24},{32,36},... | collective-permute-start | bytes 1794056 | tf_op jit(solution)/shard_map/ppermute | solution.py:289
  16.6 0.0 copy-start.2
  16.6 9.4 %collective-permute-start = (bf16[1168,256]{1,0:T(8,128)(2,1)S(1)}, bf16[1168,256]{1,0:T(8,128)(2,1)S(1)}, u32[]{:S(2)}, u32[]{:S(2)}) collective-permute-start(bf16[1168,256]{1,0:T(8,128)(2,1)S(1)} %get-tuple-element.11.pay_b.pay), channel_id=1, source_target_pairs={{0,508},{4,8},{8,4},{12,16},{16,12},{20,24},{24,20},{28,32},{32,28... | collective-permute-start | bytes 1794056 | tf_op jit(solution)/shard_map/ppermute | solution.py:279
  26.0 0.0 collective-permute-done.1.rec
  26.0 0.0 copy-start
  26.0 0.8 %copy-done = bf16[1168,256]{1,0:T(8,128)(2,1)} copy-done((bf16[1168,256]{1,0:T(8,128)(2,1)}, bf16[1168,256]{1,0:T(8,128)(2,1)S(1)}, u32[]{:S(2)}) %copy-start) | copy-done | bytes 598040
  26.8 0.0 all-to-all-done.1.refs_1_
  26.8 0.0 copy-start.1
  26.8 2.0 %collective-permute-start.2 = (bf16[4,192,768]{2,1,0:T(8,128)(2,1)S(1)}, bf16[4,192,768]{2,1,0:T(8,128)(2,1)S(1)}, u32[]{:S(2)}, u32[]{:S(2)}) collective-permute-start(bf16[4,192,768]{2,1,0:T(8,128)(2,1)S(1)} %all-to-all-done.1.refs_1_), channel_id=1, source_target_pairs={{0,4},{4,0},{8,12},{12,8},{16,20},{20,16},{24,28},{28,24},{32,36},... | collective-permute-start | bytes 3538952 | tf_op jit(solution)/shard_map/ppermute | solution.py:318
  28.9 0.0 copy-done.3
  28.9 4.2 %shard_map.123 = (f32[4,3,80,256]{3,2,1,0:T(8,128)S(1)}, f32[4,3,8,256]{3,2,1,0:T(8,128)S(1)}) custom-call(s32[1]{0:T(128)S(6)} %copy.21.count, s32[2]{0:T(128)S(1)} %copy-done.3, bf16[1168,256]{1,0:T(8,128)(2,1)S(1)} %get-tuple-element.12.pay_a.pay, bf16[1168,256]{1,0:T(8,128)(2,1)S(1)} %get-tuple-element.11.pay_b.pay), custom_call_target="tpu_custom_call" | custom-call | flops 10000000000 | bytes 1 | tf_op jit(solution)/shard_map/pallas_call | solution.py:280
  33.0 0.0 copy-done.2
  33.0 0.0 copy-done.1
  33.0 2.6 %shard_map.124 = (f32[4,3,80,256]{3,2,1,0:T(8,128)S(1)}, f32[4,3,8,256]{3,2,1,0:T(8,128)S(1)}) custom-call(s32[1]{0:T(128)S(6)} %copy.21.count, s32[2]{0:T(128)S(1)} %copy-done.2, bf16[1168,256]{1,0:T(8,128)(2,1)S(1)} %get-tuple-element.12.pay_a.pay, bf16[1168,256]{1,0:T(8,128)(2,1)S(1)} %copy-done.1, ...), custom_call_target="tpu_custom_call", output_to_operand_aliasing={{0}: (4, {}), {1}: (5, {})} | custom-call | flops 1 | bytes 1 | tf_op jit(solution)/shard_map/pallas_call | solution.py:290
  35.6 0.0 collective-permute-done.rec
  35.6 2.6 %shard_map.125 = (bf16[4,384,128]{2,1,0:T(8,128)(2,1)S(1)}, f32[4,3,80,256]{3,2,1,0:T(8,128)S(1)}, f32[4,3,8,256]{3,2,1,0:T(8,128)S(1)}) custom-call(s32[1]{0:T(128)S(6)} %copy.21.count, s32[2]{0:T(128)S(1)} %copy-done.2, bf16[1168,256]{1,0:T(8,128)(2,1)S(1)} %get-tuple-element.11.pay_b.pay, ...), custom_call_target="tpu_custom_call", output_to_operand_aliasing={{1}: (4, {}), {2}: (5, {})} | custom-call | flops 1 | bytes 1 | tf_op jit(solution)/shard_map/pallas_call | solution.py:300
  38.3 10.5 %all_to_all.10.refs_0_ = bf16[4,384,128]{2,1,0:T(8,128)(2,1)S(1)} all-to-all(bf16[4,384,128]{2,1,0:T(8,128)(2,1)S(1)} %get-tuple-element.17), channel_id=1, replica_groups=mesh['tile'=128,'head'=4] {'head'}, dimensions={0} | all-to-all | bytes 786432 | tf_op jit(solution)/shard_map/all_to_all | solution.py:316
  48.8 0.0 collective-permute-done.2.refs_2_
  48.8 1.4 %shard_map.126 = (bf16[128,768]{1,0:T(8,128)(2,1)}, bf16[128,768]{1,0:T(8,128)(2,1)}) custom-call(bf16[4,384,128]{2,1,0:T(8,128)(2,1)S(1)} %all_to_all.10.refs_0_, bf16[4,192,768]{2,1,0:T(8,128)(2,1)S(1)} %all-to-all-done.1.refs_1_, bf16[4,192,768]{2,1,0:T(8,128)(2,1)S(1)} %collective-permute-done.2.refs_2_), custom_call_target="tpu_custom_call" | custom-call | flops 1 | bytes 1 | tf_op jit(solution)/shard_map/pallas_call | solution.py:319
Async XLA Ops:
  5.2 23.6 %copy-start.3 = (s32[2]{0:T(128)S(1)}, s32[2]{0:T(128)}, u32[]{:S(2)}) copy-start(s32[2]{0:T(128)} %home.1) | copy-start | bytes 28
  5.2 21.6 %all-to-all-start.1 = ((bf16[4,192,768]{2,1,0:T(8,128)(2,1)}), bf16[4,192,768]{2,1,0:T(8,128)(2,1)S(1)}, u32[]{:S(2)}, u32[]{:S(2)}) async-start(bf16[4,192,768]{2,1,0:T(8,128)(2,1)} %get-tuple-element.18), calls=%async_computation.1 | async-start | bytes 2359296 | tf_op jit(solution)/shard_map/all_to_all | solution.py:278
  14.6 11.3 %collective-permute-start.1 = (bf16[1168,256]{1,0:T(8,128)(2,1)S(1)}, bf16[1168,256]{1,0:T(8,128)(2,1)S(1)}, u32[]{:S(2)}, u32[]{:S(2)}) collective-permute-start(bf16[1168,256]{1,0:T(8,128)(2,1)S(1)} %get-tuple-element.12.pay_a.pay), channel_id=1, source_target_pairs={{0,4},{4,0},{8,12},{12,8},{16,20},{20,16},{24,28},{28,24},{32,36},... | collective-permute-start | bytes 1794056 | tf_op jit(solution)/shard_map/ppermute | solution.py:289
  16.6 16.5 %copy-start.2 = (s32[2]{0:T(128)S(1)}, s32[2]{0:T(128)}, u32[]{:S(2)}) copy-start(s32[2]{0:T(128)} %seam.3) | copy-start | bytes 28
  16.6 19.1 %collective-permute-start = (bf16[1168,256]{1,0:T(8,128)(2,1)S(1)}, bf16[1168,256]{1,0:T(8,128)(2,1)S(1)}, u32[]{:S(2)}, u32[]{:S(2)}) collective-permute-start(bf16[1168,256]{1,0:T(8,128)(2,1)S(1)} %get-tuple-element.11.pay_b.pay), channel_id=1, source_target_pairs={{0,508},{4,8},{8,4},{12,16},{16,12},{20,24},{24,20},{28,32},{32,28... | collective-permute-start | bytes 1794056 | tf_op jit(solution)/shard_map/ppermute | solution.py:279
  26.0 0.8 %copy-start = (bf16[1168,256]{1,0:T(8,128)(2,1)}, bf16[1168,256]{1,0:T(8,128)(2,1)S(1)}, u32[]{:S(2)}) copy-start(bf16[1168,256]{1,0:T(8,128)(2,1)S(1)} %collective-permute-done.1.rec) | copy-start | bytes 1794052
  26.8 6.2 %copy-start.1 = (bf16[1168,256]{1,0:T(8,128)(2,1)S(1)}, bf16[1168,256]{1,0:T(8,128)(2,1)}, u32[]{:S(2)}) copy-start(bf16[1168,256]{1,0:T(8,128)(2,1)} %copy-done) | copy-start | bytes 1794052
  26.8 22.0 %collective-permute-start.2 = (bf16[4,192,768]{2,1,0:T(8,128)(2,1)S(1)}, bf16[4,192,768]{2,1,0:T(8,128)(2,1)S(1)}, u32[]{:S(2)}, u32[]{:S(2)}) collective-permute-start(bf16[4,192,768]{2,1,0:T(8,128)(2,1)S(1)} %all-to-all-done.1.refs_1_), channel_id=1, source_target_pairs={{0,4},{4,0},{8,12},{12,8},{16,20},{20,16},{24,28},{28,24},{32,36},... | collective-permute-start | bytes 3538952 | tf_op jit(solution)/shard_map/ppermute | solution.py:318

commit v3 on v2

v3 whole, which is shorter than its diff:
```python
import jax
import jax.numpy as jnp
from jax import lax
from jax.experimental import pallas as pl
from jax.experimental.pallas import tpu as pltpu
from jax.sharding import PartitionSpec as P

HD = 64
BS = 256
HEADS = 3
WIDTH = HEADS * HD
PAIR = 2 * WIDTH
GROUPS = 4
D = 768
NEG = -1e30
ROWS_O = HD + 16
PAY = 3 * PAIR + 16
PAY_B = PAY + 64
NT = (((1,), (1,)), ((), ()))
TN = (((0,), (0,)), ((), ()))
VMEM_LIMIT = 48 * 1024 * 1024


def dot32(a, b):
    return jnp.dot(a, b, preferred_element_type=jnp.float32)


def parity():
    return lax.axis_index("tile") % 2


def slots():
    return 1 - parity(), parity()


def write_flags(pay, slot, count, home, seam):
    lane = lax.broadcasted_iota(jnp.int32, (16, BS), 1)
    live = (slot < count[0]).astype(jnp.int32)
    flags = jnp.where(lane < 64, seam[slot] & 1, jnp.where(lane < 128, live, home[slot]))
    pay[3 * PAIR : PAY] = flags.astype(jnp.float32).astype(jnp.bfloat16)


def read_flags(pay):
    flags = pay[3 * PAIR : PAY].astype(jnp.float32)
    target, live, home = (jnp.max(flags[:, 64 * i : 64 * (i + 1)]).astype(jnp.int32) for i in range(3))
    return target, live > 0, home


def project_kernel(
    count_any, home_hbm, seam_hbm, grid, obs, w_q, w_gv, w_k, w_ov, w_g, w_o, pay_a, pay_b, spread, tok, wts, seam, home, count, sems
):
    slot_a, slot_b = slots()

    def rows(ref, block):
        return ref.at[pl.ds(pl.multiple_of(block * BS, BS), BS)]

    weights = (w_q, w_gv, w_k, w_ov)
    load_w = [pltpu.make_async_copy(w, wts.at[pl.ds(i * WIDTH, WIDTH)], sems.at[i]) for i, w in enumerate(weights)]
    load_g = pltpu.make_async_copy(grid, tok.at[pl.ds(0, 2 * BS)], sems.at[4])
    load_b = pltpu.make_async_copy(rows(obs, slot_b), tok.at[pl.ds(2 * BS, BS)], sems.at[5])
    load_a = pltpu.make_async_copy(rows(obs, slot_a), tok.at[pl.ds(3 * BS, BS)], sems.at[6])
    load_seam = pltpu.make_async_copy(seam_hbm, seam, sems.at[7])
    load_home = pltpu.make_async_copy(home_hbm, home, sems.at[10])
    load_count = pltpu.make_async_copy(count_any, count, sems.at[8])
    for copy in (load_w[0], load_w[1], load_g, load_w[2], load_w[3], load_b, load_a, load_seam, load_home, load_count):
        copy.start()

    load_s = [pltpu.make_async_copy(w, spread.at[0], sems.at[9]) for w in (w_g, w_o)]

    @pl.when(slot_b == 0)
    def _():
        load_s[0].start()

    @pl.when(slot_b == 1)
    def _():
        load_s[1].start()

    def project(i):
        w = wts[i * PAIR : (i + 1) * PAIR]
        t = tok[2 * i * BS : 2 * (i + 1) * BS]
        return lax.dot_general(w, t, NT, preferred_element_type=jnp.float32).astype(jnp.bfloat16)

    load_seam.wait()
    load_home.wait()
    load_count.wait()
    write_flags(pay_a, slot_a, count, home, seam)
    write_flags(pay_b, slot_b, count, home, seam)
    load_w[0].wait()
    load_w[1].wait()
    load_g.wait()
    x = project(0)
    for block in range(2):
        part = x[:, block * BS : (block + 1) * BS]
        pay_a[block * PAIR : (block + 1) * PAIR] = part
        pay_b[block * PAIR : (block + 1) * PAIR] = part
    load_w[2].wait()
    load_w[3].wait()
    load_b.wait()
    load_a.wait()
    x = project(1)
    pay_b[2 * PAIR : 3 * PAIR] = x[:, :BS]
    pay_a[2 * PAIR : 3 * PAIR] = x[:, BS:]
    load_s[0].wait()
    for k in range(1, GROUPS):
        spread[k] = spread[0]


def attend(tasks):
    ones = jnp.ones((ROWS_O - HD, BS), jnp.bfloat16)
    heads = [slice(h * HD, (h + 1) * HD) for h in range(HEADS)]
    scores = []
    for rows_t, columns_t, _values in tasks:
        for at in heads:
            rows = jnp.transpose(rows_t[at]) * jnp.bfloat16(0.125)
            scores.append(dot32(rows, columns_t[at]))
    parts = []
    for index, s in enumerate(scores):
        values = tasks[index // HEADS][2][heads[index % HEADS]]
        m = jnp.max(s, axis=0, keepdims=True)
        e = jnp.exp(s - m).astype(jnp.bfloat16)
        parts.append((dot32(jnp.concatenate([values, ones], axis=0), e), m))
    return [parts[HEADS * t : HEADS * (t + 1)] for t in range(len(tasks))]


def fold(acc, top, index, parts, live):
    for h, (o, m) in enumerate(parts):
        old = top[index, h, :1]
        new = jnp.where(live, jnp.maximum(old, m), old)
        weight = jnp.where(live, jnp.exp(m - new), 0.0)
        acc[index, h] = acc[index, h] * jnp.exp(old - new) + o * weight
        top[index, h] = jnp.broadcast_to(new, (8, BS))


def block_rows(ref, block):
    start = pl.multiple_of(block * PAIR, WIDTH)
    return ref[pl.ds(start, WIDTH)], ref[pl.ds(pl.multiple_of(start + WIDTH, WIDTH), WIDTH)]


def home_kernel(pay_a, pay_b, acc, top):
    tasks, blocks, lives = [], [], []
    for pay in (pay_a, pay_b):
        _target, live, block = read_flags(pay)
        q_t, gv_t = block_rows(pay, block)
        k_t, ov_t = block_rows(pay, 2)
        tasks += [(k_t, q_t, ov_t), (q_t, k_t, gv_t)]
        blocks.append(block)
        lives.append(live)
    grid_a, obs_a, grid_b, obs_b = attend(tasks)
    for index, parts in ((2, obs_a), (3, obs_b)):
        for h, (o, m) in enumerate(parts):
            acc[index, h] = o
            top[index, h] = jnp.broadcast_to(m, (8, BS))
    for block in range(2):
        used = [(b == block) & live for b, live in zip(blocks, lives)]
        for h in range(HEADS):
            pair = (grid_a[h], grid_b[h])
            new = jnp.maximum(*[jnp.where(u, m, NEG) for u, (_o, m) in zip(used, pair)])
            first, second = [o * jnp.where(u, jnp.exp(m - new), 0.0) for u, (o, m) in zip(used, pair)]
            acc[block, h] = first + second
            top[block, h] = jnp.broadcast_to(new, (8, BS))


def seam_kernel(pay_a, pay_b, rec_a, rec_b, _acc, _top, *refs):
    outs, (acc, top, mix) = refs[:-3], refs[-3:]
    tasks, blocks, lives = [], [], []
    lives_own = []
    for pay, rec in zip((pay_a, pay_b), (rec_a, rec_b)):
        target, live_own, _home = read_flags(pay)
        block_in, live_in, _home = read_flags(rec)
        lives_own.append(live_own)
        q_far, gv_far = block_rows(rec, target)
        k_far, ov_far = block_rows(rec, 2)
        q_own, _gv = block_rows(pay, block_in)
        k_own, _ov = block_rows(pay, 2)
        tasks += [(k_far, q_own, ov_far), (q_far, k_own, gv_far)]
        blocks.append(block_in)
        lives.append(live_in)
    for i, parts in enumerate(attend(tasks)):
        if i % 2 == 0:
            fold(acc, top, blocks[i // 2], parts, lives[i // 2])
        else:
            fold(acc, top, 2 + i // 2, parts, True)
    if len(outs) == 1:
        mix = outs[0]
    slot_a, slot_b = slots()
    for index in range(4):
        if index < 2:
            chunk, first, live = 2 * index, 0, True
        else:
            slot = slot_a if index == 2 else slot_b
            chunk, first, live = 2 * slot, WIDTH, lives_own[index - 2]
        for h in range(HEADS):
            o = acc[index, h]
            l = o[HD : HD + 1]
            value = (o[:HD] * jnp.where(live & (l > 0), 1.0 / jnp.where(l > 0, l, 1.0), 0.0)).astype(jnp.bfloat16)
            at = first + h * HD
            mix[chunk, at : at + HD] = value[:, :128]
            mix[chunk + 1, at : at + HD] = value[:, 128:]
    if len(outs) > 1:
        for s, out in enumerate(outs):
            out[...] = mix[(lax.axis_index("head") + s) % GROUPS]


def apply_out(mixes, first, w):
    total = None
    for k in range(GROUPS):
        rows = mixes[k, pl.ds(pl.multiple_of(first, WIDTH), WIDTH)]
        piece = lax.dot_general(rows, w[k], TN, preferred_element_type=jnp.float32)
        piece = piece.astype(jnp.bfloat16).astype(jnp.float32)
        total = piece if total is None else total + piece
    return total.astype(jnp.bfloat16)


def own_out_kernel(mixes, w_own, out):
    out[...] = apply_out(mixes, parity() * WIDTH, w_own)


def other_out_kernel(mixes, w_other, own, grid_out, obs_out):
    other = apply_out(mixes, (1 - parity()) * WIDTH, w_other)
    first = parity() == 0
    grid_out[...] = jnp.where(first, own[...], other)
    obs_out[...] = jnp.where(first, other, own[...])


SMEM = pl.BlockSpec(memory_space=pltpu.SMEM)
VMEM = pl.BlockSpec(memory_space=pltpu.VMEM)
ANY = pl.BlockSpec(memory_space=pltpu.HBM)
PARAMS = pltpu.CompilerParams(vmem_limit_bytes=VMEM_LIMIT)


def in_hbm(x):
    return pltpu.with_memory_space_constraint(x, pltpu.HBM)


def in_vmem(x):
    return pltpu.with_memory_space_constraint(x, pltpu.VMEM)


def cost(flops, moved, exps=0):
    return pl.CostEstimate(flops=flops, bytes_accessed=moved, transcendentals=exps)


MIX_BY_PERMUTE = False


def body(
    grid_tokens, obs_tokens, w_query, w_gridval, w_key, w_obsval, w_gridout, w_obsout, obs_count, home_block, seam_block
):
    tiles = lax.axis_size("tile")
    swap_a = [(i, i ^ 1) for i in range(tiles)]
    swap_b = [(i, (i + 1) % tiles if i % 2 else (i - 1) % tiles) for i in range(tiles)]
    f32, bf16 = jnp.float32, jnp.bfloat16
    pay_shape = pltpu.VMEM((PAY, BS), bf16)
    pay_b_shape = pltpu.VMEM((PAY_B, BS), bf16)
    acc_shape = pltpu.VMEM((4, HEADS, ROWS_O, BS), f32)
    top_shape = pltpu.VMEM((4, HEADS, 8, BS), f32)
    mix_shape = jax.ShapeDtypeStruct((PAIR, 128), bf16)
    mixes_shape = pltpu.VMEM((GROUPS, PAIR, 128), bf16)
    w_shape = pltpu.VMEM((GROUPS, WIDTH, D), bf16)
    out_shape = jax.ShapeDtypeStruct((128, D), bf16)

    pay_a, pay_b, w_spread = pl.pallas_call(
        project_kernel,
        out_shape=(pay_shape, pay_b_shape, w_shape),
        in_specs=[pl.BlockSpec(memory_space=pl.ANY)] + [ANY] * 10,
        out_specs=(VMEM, VMEM, VMEM),
        scratch_shapes=[
            pltpu.VMEM((4 * BS, D), bf16),
            pltpu.VMEM((4 * WIDTH, D), bf16),
            pltpu.SMEM((2,), jnp.int32),
            pltpu.SMEM((2,), jnp.int32),
            pltpu.SMEM((1,), jnp.int32),
            pltpu.SemaphoreType.DMA((11,)),
        ],
        compiler_params=PARAMS,
        cost_estimate=cost(1, 1),
    )(
        obs_count,
        *map(
            in_hbm,
            (home_block, seam_block, grid_tokens, obs_tokens, w_query.T, w_gridval.T, w_key.T, w_obsval.T, w_gridout, w_obsout),
        ),
    )
    w_own = lax.all_to_all(w_spread, "head", split_axis=0, concat_axis=0, tiled=True)
    rec_b = lax.ppermute(pay_b, "tile", swap_b)
    acc, top = pl.pallas_call(
        home_kernel,
        out_shape=(acc_shape, top_shape),
        in_specs=[VMEM] * 2,
        out_specs=(VMEM, VMEM),
        compiler_params=PARAMS,
        cost_estimate=cost(3 * 10**9, 1),
    )(pay_a, pay_b)
    pay_a2 = pay_a
    rec_a = lax.ppermute(pay_a2, "tile", swap_a)
    count = GROUPS if MIX_BY_PERMUTE else 1
    mixes = pl.pallas_call(
        seam_kernel,
        out_shape=((mix_shape,) * GROUPS if MIX_BY_PERMUTE else (mixes_shape,)) + (acc_shape, top_shape),
        in_specs=[VMEM] * 6,
        out_specs=(VMEM,) * (count + 2),
        input_output_aliases={4: count, 5: count + 1},
        scratch_shapes=[pltpu.VMEM(mixes_shape.shape if MIX_BY_PERMUTE else (1, 16, 128), bf16)],
        compiler_params=PARAMS,
        cost_estimate=cost(1, 1),
    )(pay_a, pay_b, in_vmem(rec_a), in_vmem(rec_b), acc, top)
    late = mixes[0]
    late = mixes[0]
    if MIX_BY_PERMUTE:
        mixes = [mixes[0]] + [
            lax.ppermute(mixes[s], "head", [(i, (i + s) % GROUPS) for i in range(GROUPS)]) for s in (1, 2, 3)
        ]
    else:
        mixes = [lax.all_to_all(mixes[0], "head", split_axis=0, concat_axis=0, tiled=True)]
    w_own2, *_ = lax.optimization_barrier((w_own, late))
    w_other = lax.ppermute(w_own2, "tile", swap_a)
    own = pl.pallas_call(
        own_out_kernel,
        out_shape=pltpu.VMEM(out_shape.shape, bf16),
        in_specs=[VMEM] * 2,
        out_specs=VMEM,
        compiler_params=PARAMS,
        cost_estimate=cost(10**10, 1),
    )(in_vmem(mixes[0]), in_vmem(w_own))
    return pl.pallas_call(
        other_out_kernel,
        out_shape=(out_shape, out_shape),
        in_specs=[VMEM] * 3,
        out_specs=(VMEM, VMEM),
        compiler_params=PARAMS,
        cost_estimate=cost(1, 1),
    )(in_vmem(mixes[0]), in_vmem(w_other), own)


def solution(mesh):
    return jax.shard_map(
        body,
        mesh=mesh,
        in_specs=(
            P("tile", None),
            P("tile", None),
            P(None, "head"),
            P(None, "head"),
            P(None, "head"),
            P(None, "head"),
            P("head", None),
            P("head", None),
            P("tile"),
            P("tile"),
            P("tile"),
        ),
        out_specs=(P(("tile", "head"), None), P(("tile", "head"), None)),
        check_vma=False,
    )
```

time: 50.5 us -> 45.3 us (0.90)
  blocking collectives: 10.5 us -> 0 us
  waiting for transfers between devices: 0.01 us -> 8.75 us
  Pallas kernels: 14.7 us -> 8.66 us
  starting transfers between devices: 22.7 us -> 26.2 us
  local copies, waits for them, and re-layouts: 0.83 us -> 0 us
    all_to_all x1 -> x0, blocking collectives: 10.5 us -> none  [body(): lax.all_to_all(mixes[0], 'head', split_axis=0, concat_axis=0, tiled=True)]
    pallas_call x5, Pallas kernels: 14.7 us -> 8.66 us  [the longest x1 3.51 us: body(): pl.pallas_call(project_kernel, out_shape=(pay_shape, pay_b_shape, w_shape...]
    all_to_all x0 -> x1, starting transfers between devices: none -> 4.8 us  [body(): lax.all_to_all(mixes[0], 'head', split_axis=0, concat_axis=0, tiled=True)]
    ppermute x1, waiting for transfers between devices: 0.01 us -> 4.08 us  [body(): rec_b = lax.ppermute(pay_b, 'tile', swap_b)]
    all_to_all x0 -> x1, waiting for transfers between devices: none -> 4.01 us  [body(): lax.all_to_all(mixes[0], 'head', split_axis=0, concat_axis=0, tiled=True)]
    ppermute x1, starting transfers between devices: 9.38 us -> 8.14 us  [body(): rec_b = lax.ppermute(pay_b, 'tile', swap_b)]
    unnamed x8 -> x0, local copies, waits for them, and re-layouts: 0.83 us -> none
    ppermute x1, waiting for transfers between devices: 0.01 us -> 0.66 us  [body(): rec_a = lax.ppermute(pay_a2, 'tile', swap_a)]
  transfers between devices with their start and end apart: 4 -> 5, of which waited for: 0 -> 3; matrix products, arithmetic and copies ran while one was open for 0% -> 0% of each run, Pallas kernels for 19% -> 9%
where the time goes in v3:
time: 45.3 us; the launch traced here: 44.9 us
  starting transfers between devices  26.2 us (58%)
  waiting for transfers between devices  8.75 us (19%)
  Pallas kernels  8.66 us (19%)
  between operations  1.33 us (3%)
    all_to_all x1, starting transfers between devices, body(): lax.all_to_all(w_spread, 'head', split_axis=0, concat_axis=0, tiled=True)  9.42 us
    ppermute x1, starting transfers between devices, body(): rec_b = lax.ppermute(pay_b, 'tile', swap_b)  8.14 us
    all_to_all x1, starting transfers between devices, body(): lax.all_to_all(mixes[0], 'head', split_axis=0, concat_axis=0, tiled=True)  4.8 us
    ppermute x1, waiting for transfers between devices, body(): rec_b = lax.ppermute(pay_b, 'tile', swap_b)  4.08 us
    all_to_all x1, waiting for transfers between devices, body(): lax.all_to_all(mixes[0], 'head', split_axis=0, concat_axis=0, tiled=True)  4.01 us
    pallas_call x1, Pallas kernels, body(): pl.pallas_call(project_kernel, out_shape=(pay_shape, pay_b_shape, w_shape...  3.51 us
    pallas_call x1, Pallas kernels, body(): pl.pallas_call(seam_kernel, out_shape=((mix_shape,) * GROUPS if MIX_BY_PE...  2.23 us
    ppermute x1, starting transfers between devices, body(): rec_a = lax.ppermute(pay_a2, 'tile', swap_a)  1.92 us
  transfers between devices with their start and end apart: 5, of which 3 were waited for; matrix products, arithmetic and copies ran while one was open for 0% of the time, Pallas kernels for 9%

profile of v3, /device:TPU:2, one launch (start us, length us, event | category | flops | bytes accessed | tf_op | source)
XLA Modules:
  0.0 44.9 jit_solution(6263030074556147780)
XLA Ops:
  1.3 3.5 %shard_map.122 = (bf16[1168,256]{1,0:T(8,128)(2,1)S(1)}, bf16[1232,256]{1,0:T(8,128)(2,1)S(1)}, bf16[4,192,768]{2,1,0:T(8,128)(2,1)}) custom-call(s32[1]{0:T(128)S(6)} %copy.17.count_any, s32[2]{0:T(128)} %home_hbm.1, s32[2]{0:T(128)} %seam_hbm.1, bf16[512,768]{1,0:T(8,128)(2,1)} %grid.1, bf16[512,768]{1,0:T(8,128)(2,1)} %obs.1, bf16[192,768]{1,0:T(8,128)(2,1)} %bitcast.4, ...), custom_call_target="tpu_custom_call" | custom-call | flops 1 | bytes 1 | tf_op jit(solution)/shard_map/pallas_call | solution.py:262
  4.8 9.4 %all-to-all-start.1 = ((bf16[4,192,768]{2,1,0:T(8,128)(2,1)}), bf16[4,192,768]{2,1,0:T(8,128)(2,1)S(1)}, u32[]{:S(2)}, u32[]{:S(2)}) async-start(bf16[4,192,768]{2,1,0:T(8,128)(2,1)} %get-tuple-element.14), calls=%async_computation.1 | async-start | bytes 2359296 | tf_op jit(solution)/shard_map/all_to_all | solution.py:284
  14.2 8.1 %collective-permute-start.1 = (bf16[1232,256]{1,0:T(8,128)(2,1)S(1)}, bf16[1232,256]{1,0:T(8,128)(2,1)S(1)}, u32[]{:S(2)}, u32[]{:S(2)}) collective-permute-start(bf16[1232,256]{1,0:T(8,128)(2,1)S(1)} %get-tuple-element.10.pay_b), channel_id=1, source_target_pairs={{0,508},{4,8},{8,4},{12,16},{16,12},{20,24},{24,20},{28,32},{32,28... | collective-permute-start | bytes 1892360 | tf_op jit(solution)/shard_map/ppermute | solution.py:285
  22.4 1.9 %collective-permute-start = (bf16[1168,256]{1,0:T(8,128)(2,1)S(1)}, bf16[1168,256]{1,0:T(8,128)(2,1)S(1)}, u32[]{:S(2)}, u32[]{:S(2)}) collective-permute-start(bf16[1168,256]{1,0:T(8,128)(2,1)S(1)} %get-tuple-element.9.pay_a), channel_id=1, source_target_pairs={{0,4},{4,0},{8,12},{12,8},{16,20},{20,16},{24,28},{28,24},{32,36},... | collective-permute-start | bytes 1794056 | tf_op jit(solution)/shard_map/ppermute | solution.py:295
  24.3 1.3 %shard_map.123 = (f32[4,3,80,256]{3,2,1,0:T(8,128)S(1)}, f32[4,3,8,256]{3,2,1,0:T(8,128)S(1)}) custom-call(bf16[1168,256]{1,0:T(8,128)(2,1)S(1)} %get-tuple-element.9.pay_a, bf16[1232,256]{1,0:T(8,128)(2,1)S(1)} %get-tuple-element.10.pay_b), custom_call_target="tpu_custom_call" | custom-call | flops 3000000000 | bytes 1 | tf_op jit(solution)/shard_map/pallas_call | solution.py:286
  25.6 0.7 %collective-permute-done.rec_a = bf16[1168,256]{1,0:T(8,128)(2,1)S(1)} collective-permute-done((bf16[1168,256]{1,0:T(8,128)(2,1)S(1)}, bf16[1168,256]{1,0:T(8,128)(2,1)S(1)}, u32[]{:S(2)}, u32[]{:S(2)}) %collective-permute-start) | collective-permute-done | bytes 598048 | tf_op jit(solution)/shard_map/ppermute | solution.py:295
  26.3 4.1 %collective-permute-done.1.rec_b = bf16[1232,256]{1,0:T(8,128)(2,1)S(1)} collective-permute-done((bf16[1232,256]{1,0:T(8,128)(2,1)S(1)}, bf16[1232,256]{1,0:T(8,128)(2,1)S(1)}, u32[]{:S(2)}, u32[]{:S(2)}) %collective-permute-start.1) | collective-permute-done | bytes 630816 | tf_op jit(solution)/shard_map/ppermute | solution.py:285
  30.4 2.2 %shard_map.124 = (bf16[4,384,128]{2,1,0:T(8,128)(2,1)}, f32[4,3,80,256]{3,2,1,0:T(8,128)S(1)}, f32[4,3,8,256]{3,2,1,0:T(8,128)S(1)}) custom-call(bf16[1168,256]{1,0:T(8,128)(2,1)S(1)} %get-tuple-element.9.pay_a, bf16[1232,256]{1,0:T(8,128)(2,1)S(1)} %get-tuple-element.10.pay_b, ...), custom_call_target="tpu_custom_call", output_to_operand_aliasing={{1}: (4, {}), {2}: (5, {})} | custom-call | flops 1 | bytes 1 | tf_op jit(solution)/shard_map/pallas_call | solution.py:297
  32.6 0.0 all-to-all-done.1.w_own
  32.6 4.8 %all-to-all-start = ((bf16[4,384,128]{2,1,0:T(8,128)(2,1)}), bf16[4,384,128]{2,1,0:T(8,128)(2,1)S(1)}, u32[]{:S(2)}, u32[]{:S(2)}) async-start(bf16[4,384,128]{2,1,0:T(8,128)(2,1)} %get-tuple-element.13), calls=%async_computation | async-start | bytes 786432 | tf_op jit(solution)/shard_map/all_to_all | solution.py:314
  37.4 1.9 %collective-permute-start.2 = (bf16[4,192,768]{2,1,0:T(8,128)(2,1)S(1)}, bf16[4,192,768]{2,1,0:T(8,128)(2,1)S(1)}, u32[]{:S(2)}, u32[]{:S(2)}) collective-permute-start(bf16[4,192,768]{2,1,0:T(8,128)(2,1)S(1)} %all-to-all-done.1.w_own), channel_id=1, source_target_pairs={{0,4},{4,0},{8,12},{12,8},{16,20},{20,16},{24,28},{28,24},{32,36},... | collective-permute-start | bytes 3538952 | tf_op jit(solution)/shard_map/ppermute | solution.py:316
  39.3 4.0 %all-to-all-done.mixes = bf16[4,384,128]{2,1,0:T(8,128)(2,1)S(1)} async-done(((bf16[4,384,128]{2,1,0:T(8,128)(2,1)}), bf16[4,384,128]{2,1,0:T(8,128)(2,1)S(1)}, u32[]{:S(2)}, u32[]{:S(2)}) %all-to-all-start) | async-done | bytes 393248 | tf_op jit(solution)/shard_map/all_to_all | solution.py:314
  43.3 0.4 shard_map.125.own
  43.7 0.0 collective-permute-done.2.w_other
  43.7 1.2 %shard_map.126 = (bf16[128,768]{1,0:T(8,128)(2,1)}, bf16[128,768]{1,0:T(8,128)(2,1)}) custom-call(bf16[4,384,128]{2,1,0:T(8,128)(2,1)S(1)} %all-to-all-done.mixes, bf16[4,192,768]{2,1,0:T(8,128)(2,1)S(1)} %collective-permute-done.2.w_other, bf16[128,768]{1,0:T(8,128)(2,1)S(1)} %shard_map.125.own), custom_call_target="tpu_custom_call" | custom-call | flops 1 | bytes 1 | tf_op jit(solution)/shard_map/pallas_call | solution.py:325
Async XLA Ops:
  4.8 27.8 %all-to-all-start.1 = ((bf16[4,192,768]{2,1,0:T(8,128)(2,1)}), bf16[4,192,768]{2,1,0:T(8,128)(2,1)S(1)}, u32[]{:S(2)}, u32[]{:S(2)}) async-start(bf16[4,192,768]{2,1,0:T(8,128)(2,1)} %get-tuple-element.14), calls=%async_computation.1 | async-start | bytes 2359296 | tf_op jit(solution)/shard_map/all_to_all | solution.py:284
  14.2 16.1 %collective-permute-start.1 = (bf16[1232,256]{1,0:T(8,128)(2,1)S(1)}, bf16[1232,256]{1,0:T(8,128)(2,1)S(1)}, u32[]{:S(2)}, u32[]{:S(2)}) collective-permute-start(bf16[1232,256]{1,0:T(8,128)(2,1)S(1)} %get-tuple-element.10.pay_b), channel_id=1, source_target_pairs={{0,508},{4,8},{8,4},{12,16},{16,12},{20,24},{24,20},{28,32},{32,28... | collective-permute-start | bytes 1892360 | tf_op jit(solution)/shard_map/ppermute | solution.py:285
  22.4 3.9 %collective-permute-start = (bf16[1168,256]{1,0:T(8,128)(2,1)S(1)}, bf16[1168,256]{1,0:T(8,128)(2,1)S(1)}, u32[]{:S(2)}, u32[]{:S(2)}) collective-permute-start(bf16[1168,256]{1,0:T(8,128)(2,1)S(1)} %get-tuple-element.9.pay_a), channel_id=1, source_target_pairs={{0,4},{4,0},{8,12},{12,8},{16,20},{20,16},{24,28},{28,24},{32,36},... | collective-permute-start | bytes 1794056 | tf_op jit(solution)/shard_map/ppermute | solution.py:295
  32.6 10.7 %all-to-all-start = ((bf16[4,384,128]{2,1,0:T(8,128)(2,1)}), bf16[4,384,128]{2,1,0:T(8,128)(2,1)S(1)}, u32[]{:S(2)}, u32[]{:S(2)}) async-start(bf16[4,384,128]{2,1,0:T(8,128)(2,1)} %get-tuple-element.13), calls=%async_computation | async-start | bytes 786432 | tf_op jit(solution)/shard_map/all_to_all | solution.py:314
  37.4 6.3 %collective-permute-start.2 = (bf16[4,192,768]{2,1,0:T(8,128)(2,1)S(1)}, bf16[4,192,768]{2,1,0:T(8,128)(2,1)S(1)}, u32[]{:S(2)}, u32[]{:S(2)}) collective-permute-start(bf16[4,192,768]{2,1,0:T(8,128)(2,1)S(1)} %all-to-all-done.1.w_own), channel_id=1, source_target_pairs={{0,4},{4,0},{8,12},{12,8},{16,20},{20,16},{24,28},{28,24},{32,36},... | collective-permute-start | bytes 3538952 | tf_op jit(solution)/shard_map/ppermute | solution.py:316

commit v4 on v3

--- a/solution.py
+++ b/solution.py
@@ -15,7 +15,7 @@
 NEG = -1e30
 ROWS_O = HD + 16
 PAY = 3 * PAIR + 16
-PAY_B = PAY + 64
+PAY_B = PAY + 16
 NT = (((1,), (1,)), ((), ()))
 TN = (((0,), (0,)), ((), ()))
 VMEM_LIMIT = 48 * 1024 * 1024
@@ -47,7 +47,7 @@
 
 
 def project_kernel(
-    count_any, home_hbm, seam_hbm, grid, obs, w_q, w_gv, w_k, w_ov, w_g, w_o, pay_a, pay_b, spread, tok, wts, seam, home, count, sems
+    count_any, home_hbm, seam_hbm, grid, obs, w_q, w_gv, w_k, w_ov, w_g, w_o, pay_a, pay_b, spread, tok, wts, wide, seam, home, count, sems
 ):
     slot_a, slot_b = slots()
 
@@ -65,7 +65,7 @@
     for copy in (load_w[0], load_w[1], load_g, load_w[2], load_w[3], load_b, load_a, load_seam, load_home, load_count):
         copy.start()
 
-    load_s = [pltpu.make_async_copy(w, spread.at[0], sems.at[9]) for w in (w_g, w_o)]
+    load_s = [pltpu.make_async_copy(w, wide, sems.at[9]) for w in (w_g, w_o)]
 
     @pl.when(slot_b == 0)
     def _():
@@ -80,6 +80,10 @@
         t = tok[2 * i * BS : 2 * (i + 1) * BS]
         return lax.dot_general(w, t, NT, preferred_element_type=jnp.float32).astype(jnp.bfloat16)
 
+    load_s[0].wait()
+    send_s = [pltpu.make_async_copy(wide, spread.at[k], sems.at[11 + k]) for k in range(GROUPS)]
+    for copy in send_s:
+        copy.start()
     load_seam.wait()
     load_home.wait()
     load_count.wait()
@@ -100,9 +104,8 @@
     x = project(1)
     pay_b[2 * PAIR : 3 * PAIR] = x[:, :BS]
     pay_a[2 * PAIR : 3 * PAIR] = x[:, BS:]
-    load_s[0].wait()
-    for k in range(1, GROUPS):
-        spread[k] = spread[0]
+    for copy in send_s:
+        copy.wait()
 
 
 def attend(tasks):
@@ -256,21 +259,22 @@
     top_shape = pltpu.VMEM((4, HEADS, 8, BS), f32)
     mix_shape = jax.ShapeDtypeStruct((PAIR, 128), bf16)
     mixes_shape = pltpu.VMEM((GROUPS, PAIR, 128), bf16)
-    w_shape = pltpu.VMEM((GROUPS, WIDTH, D), bf16)
+    w_shape = pltpu.HBM((GROUPS, WIDTH, D), bf16)
     out_shape = jax.ShapeDtypeStruct((128, D), bf16)
 
     pay_a, pay_b, w_spread = pl.pallas_call(
         project_kernel,
         out_shape=(pay_shape, pay_b_shape, w_shape),
         in_specs=[pl.BlockSpec(memory_space=pl.ANY)] + [ANY] * 10,
-        out_specs=(VMEM, VMEM, VMEM),
+        out_specs=(VMEM, VMEM, ANY),
         scratch_shapes=[
             pltpu.VMEM((4 * BS, D), bf16),
             pltpu.VMEM((4 * WIDTH, D), bf16),
+            pltpu.VMEM((WIDTH, D), bf16),
             pltpu.SMEM((2,), jnp.int32),
             pltpu.SMEM((2,), jnp.int32),
             pltpu.SMEM((1,), jnp.int32),
-            pltpu.SemaphoreType.DMA((11,)),
+            pltpu.SemaphoreType.DMA((11 + GROUPS,)),
         ],
         compiler_params=PARAMS,
         cost_estimate=cost(1, 1),

time: 45.3 us -> 44.5 us (0.982)
  Pallas kernels: 8.66 us -> 8.14 us
    pallas_call x1, Pallas kernels: 3.51 us -> 2.98 us  [body(): pl.pallas_call(project_kernel, out_shape=(pay_shape, pay_b_shape, w_shape...]
where the time goes in v4:
time: 44.5 us; the launch traced here: 44.1 us
  starting transfers between devices  26.2 us (59%)
  waiting for transfers between devices  8.49 us (19%)
  Pallas kernels  8.14 us (18%)
  between operations  1.33 us (3%)
    all_to_all x1, starting transfers between devices, body(): lax.all_to_all(w_spread, 'head', split_axis=0, concat_axis=0, tiled=True)  9.42 us
    ppermute x1, starting transfers between devices, body(): rec_b = lax.ppermute(pay_b, 'tile', swap_b)  8.14 us
    all_to_all x1, starting transfers between devices, body(): lax.all_to_all(mixes[0], 'head', split_axis=0, concat_axis=0, tiled=True)  4.8 us
    all_to_all x1, waiting for transfers between devices, body(): lax.all_to_all(mixes[0], 'head', split_axis=0, concat_axis=0, tiled=True)  4.01 us
    ppermute x1, waiting for transfers between devices, body(): rec_b = lax.ppermute(pay_b, 'tile', swap_b)  3.82 us
    pallas_call x1, Pallas kernels, body(): pl.pallas_call(project_kernel, out_shape=(pay_shape, pay_b_shape, w_shape...  2.98 us
    pallas_call x1, Pallas kernels, body(): pl.pallas_call(seam_kernel, out_shape=((mix_shape,) * GROUPS if MIX_BY_PE...  2.23 us
    ppermute x1, starting transfers between devices, body(): rec_a = lax.ppermute(pay_a2, 'tile', swap_a)  1.92 us
  transfers between devices with their start and end apart: 5, of which 3 were waited for; matrix products, arithmetic and copies ran while one was open for 0% of the time, Pallas kernels for 9%

profile of v4, /device:TPU:2, one launch (start us, length us, event | category | flops | bytes accessed | tf_op | source)
XLA Modules:
  0.0 44.1 jit_solution(8966477504978647842)
XLA Ops:
  1.3 3.0 %shard_map.122 = (bf16[1168,256]{1,0:T(8,128)(2,1)S(1)}, bf16[1184,256]{1,0:T(8,128)(2,1)S(1)}, bf16[4,192,768]{2,1,0:T(8,128)(2,1)}) custom-call(s32[1]{0:T(128)S(6)} %copy.17.count_any, s32[2]{0:T(128)} %home_hbm.1, s32[2]{0:T(128)} %seam_hbm.1, bf16[512,768]{1,0:T(8,128)(2,1)} %grid.1, bf16[512,768]{1,0:T(8,128)(2,1)} %obs.1, bf16[192,768]{1,0:T(8,128)(2,1)} %bitcast.4, ...), custom_call_target="tpu_custom_call" | custom-call | flops 1 | bytes 1 | tf_op jit(solution)/shard_map/pallas_call | solution.py:265
  4.3 9.4 %all-to-all-start.1 = ((bf16[4,192,768]{2,1,0:T(8,128)(2,1)}), bf16[4,192,768]{2,1,0:T(8,128)(2,1)S(1)}, u32[]{:S(2)}, u32[]{:S(2)}) async-start(bf16[4,192,768]{2,1,0:T(8,128)(2,1)} %get-tuple-element.14), calls=%async_computation.1 | async-start | bytes 2359296 | tf_op jit(solution)/shard_map/all_to_all | solution.py:288
  13.7 8.1 %collective-permute-start.1 = (bf16[1184,256]{1,0:T(8,128)(2,1)S(1)}, bf16[1184,256]{1,0:T(8,128)(2,1)S(1)}, u32[]{:S(2)}, u32[]{:S(2)}) collective-permute-start(bf16[1184,256]{1,0:T(8,128)(2,1)S(1)} %get-tuple-element.10.pay_b), channel_id=1, source_target_pairs={{0,508},{4,8},{8,4},{12,16},{16,12},{20,24},{24,20},{28,32},{32,28... | collective-permute-start | bytes 1818632 | tf_op jit(solution)/shard_map/ppermute | solution.py:289
  21.8 1.9 %collective-permute-start = (bf16[1168,256]{1,0:T(8,128)(2,1)S(1)}, bf16[1168,256]{1,0:T(8,128)(2,1)S(1)}, u32[]{:S(2)}, u32[]{:S(2)}) collective-permute-start(bf16[1168,256]{1,0:T(8,128)(2,1)S(1)} %get-tuple-element.9.pay_a), channel_id=1, source_target_pairs={{0,4},{4,0},{8,12},{12,8},{16,20},{20,16},{24,28},{28,24},{32,36},... | collective-permute-start | bytes 1794056 | tf_op jit(solution)/shard_map/ppermute | solution.py:299
  23.8 1.3 %shard_map.123 = (f32[4,3,80,256]{3,2,1,0:T(8,128)S(1)}, f32[4,3,8,256]{3,2,1,0:T(8,128)S(1)}) custom-call(bf16[1168,256]{1,0:T(8,128)(2,1)S(1)} %get-tuple-element.9.pay_a, bf16[1184,256]{1,0:T(8,128)(2,1)S(1)} %get-tuple-element.10.pay_b), custom_call_target="tpu_custom_call" | custom-call | flops 3000000000 | bytes 1 | tf_op jit(solution)/shard_map/pallas_call | solution.py:290
  25.1 0.7 %collective-permute-done.rec_a = bf16[1168,256]{1,0:T(8,128)(2,1)S(1)} collective-permute-done((bf16[1168,256]{1,0:T(8,128)(2,1)S(1)}, bf16[1168,256]{1,0:T(8,128)(2,1)S(1)}, u32[]{:S(2)}, u32[]{:S(2)}) %collective-permute-start) | collective-permute-done | bytes 598048 | tf_op jit(solution)/shard_map/ppermute | solution.py:299
  25.7 3.8 %collective-permute-done.1.rec_b = bf16[1184,256]{1,0:T(8,128)(2,1)S(1)} collective-permute-done((bf16[1184,256]{1,0:T(8,128)(2,1)S(1)}, bf16[1184,256]{1,0:T(8,128)(2,1)S(1)}, u32[]{:S(2)}, u32[]{:S(2)}) %collective-permute-start.1) | collective-permute-done | bytes 606240 | tf_op jit(solution)/shard_map/ppermute | solution.py:289
  29.6 2.2 %shard_map.124 = (bf16[4,384,128]{2,1,0:T(8,128)(2,1)}, f32[4,3,80,256]{3,2,1,0:T(8,128)S(1)}, f32[4,3,8,256]{3,2,1,0:T(8,128)S(1)}) custom-call(bf16[1168,256]{1,0:T(8,128)(2,1)S(1)} %get-tuple-element.9.pay_a, bf16[1184,256]{1,0:T(8,128)(2,1)S(1)} %get-tuple-element.10.pay_b, ...), custom_call_target="tpu_custom_call", output_to_operand_aliasing={{1}: (4, {}), {2}: (5, {})} | custom-call | flops 1 | bytes 1 | tf_op jit(solution)/shard_map/pallas_call | solution.py:301
  31.8 0.0 all-to-all-done.1.w_own
  31.8 4.8 %all-to-all-start = ((bf16[4,384,128]{2,1,0:T(8,128)(2,1)}), bf16[4,384,128]{2,1,0:T(8,128)(2,1)S(1)}, u32[]{:S(2)}, u32[]{:S(2)}) async-start(bf16[4,384,128]{2,1,0:T(8,128)(2,1)} %get-tuple-element.13), calls=%async_computation | async-start | bytes 786432 | tf_op jit(solution)/shard_map/all_to_all | solution.py:318
  36.6 1.9 %collective-permute-start.2 = (bf16[4,192,768]{2,1,0:T(8,128)(2,1)S(1)}, bf16[4,192,768]{2,1,0:T(8,128)(2,1)S(1)}, u32[]{:S(2)}, u32[]{:S(2)}) collective-permute-start(bf16[4,192,768]{2,1,0:T(8,128)(2,1)S(1)} %all-to-all-done.1.w_own), channel_id=1, source_target_pairs={{0,4},{4,0},{8,12},{12,8},{16,20},{20,16},{24,28},{28,24},{32,36},... | collective-permute-start | bytes 3538952 | tf_op jit(solution)/shard_map/ppermute | solution.py:320
  38.5 4.0 %all-to-all-done.mixes = bf16[4,384,128]{2,1,0:T(8,128)(2,1)S(1)} async-done(((bf16[4,384,128]{2,1,0:T(8,128)(2,1)}), bf16[4,384,128]{2,1,0:T(8,128)(2,1)S(1)}, u32[]{:S(2)}, u32[]{:S(2)}) %all-to-all-start) | async-done | bytes 393248 | tf_op jit(solution)/shard_map/all_to_all | solution.py:318
  42.5 0.4 shard_map.125.own
  43.0 0.0 collective-permute-done.2.w_other
  43.0 1.2 %shard_map.126 = (bf16[128,768]{1,0:T(8,128)(2,1)}, bf16[128,768]{1,0:T(8,128)(2,1)}) custom-call(bf16[4,384,128]{2,1,0:T(8,128)(2,1)S(1)} %all-to-all-done.mixes, bf16[4,192,768]{2,1,0:T(8,128)(2,1)S(1)} %collective-permute-done.2.w_other, bf16[128,768]{1,0:T(8,128)(2,1)S(1)} %shard_map.125.own), custom_call_target="tpu_custom_call" | custom-call | flops 1 | bytes 1 | tf_op jit(solution)/shard_map/pallas_call | solution.py:329
Async XLA Ops:
  4.3 27.5 %all-to-all-start.1 = ((bf16[4,192,768]{2,1,0:T(8,128)(2,1)}), bf16[4,192,768]{2,1,0:T(8,128)(2,1)S(1)}, u32[]{:S(2)}, u32[]{:S(2)}) async-start(bf16[4,192,768]{2,1,0:T(8,128)(2,1)} %get-tuple-element.14), calls=%async_computation.1 | async-start | bytes 2359296 | tf_op jit(solution)/shard_map/all_to_all | solution.py:288
  13.7 15.9 %collective-permute-start.1 = (bf16[1184,256]{1,0:T(8,128)(2,1)S(1)}, bf16[1184,256]{1,0:T(8,128)(2,1)S(1)}, u32[]{:S(2)}, u32[]{:S(2)}) collective-permute-start(bf16[1184,256]{1,0:T(8,128)(2,1)S(1)} %get-tuple-element.10.pay_b), channel_id=1, source_target_pairs={{0,508},{4,8},{8,4},{12,16},{16,12},{20,24},{24,20},{28,32},{32,28... | collective-permute-start | bytes 1818632 | tf_op jit(solution)/shard_map/ppermute | solution.py:289
  21.8 3.9 %collective-permute-start = (bf16[1168,256]{1,0:T(8,128)(2,1)S(1)}, bf16[1168,256]{1,0:T(8,128)(2,1)S(1)}, u32[]{:S(2)}, u32[]{:S(2)}) collective-permute-start(bf16[1168,256]{1,0:T(8,128)(2,1)S(1)} %get-tuple-element.9.pay_a), channel_id=1, source_target_pairs={{0,4},{4,0},{8,12},{12,8},{16,20},{20,16},{24,28},{28,24},{32,36},... | collective-permute-start | bytes 1794056 | tf_op jit(solution)/shard_map/ppermute | solution.py:299
  31.8 10.7 %all-to-all-start = ((bf16[4,384,128]{2,1,0:T(8,128)(2,1)}), bf16[4,384,128]{2,1,0:T(8,128)(2,1)S(1)}, u32[]{:S(2)}, u32[]{:S(2)}) async-start(bf16[4,384,128]{2,1,0:T(8,128)(2,1)} %get-tuple-element.13), calls=%async_computation | async-start | bytes 786432 | tf_op jit(solution)/shard_map/all_to_all | solution.py:318
  36.6 6.4 %collective-permute-start.2 = (bf16[4,192,768]{2,1,0:T(8,128)(2,1)S(1)}, bf16[4,192,768]{2,1,0:T(8,128)(2,1)S(1)}, u32[]{:S(2)}, u32[]{:S(2)}) collective-permute-start(bf16[4,192,768]{2,1,0:T(8,128)(2,1)S(1)} %all-to-all-done.1.w_own), channel_id=1, source_target_pairs={{0,4},{4,0},{8,12},{12,8},{16,20},{20,16},{24,28},{28,24},{32,36},... | collective-permute-start | bytes 3538952 | tf_op jit(solution)/shard_map/ppermute | solution.py:320

commit v5 on v4

--- a/solution.py
+++ b/solution.py
@@ -129,8 +129,8 @@
     for h, (o, m) in enumerate(parts):
         old = top[index, h, :1]
         new = jnp.where(live, jnp.maximum(old, m), old)
-        weight = jnp.where(live, jnp.exp(m - new), 0.0)
-        acc[index, h] = acc[index, h] * jnp.exp(old - new) + o * weight
+        more = jnp.where(live, o * jnp.exp(m - new), 0.0)
+        acc[index, h] = acc[index, h] * jnp.exp(old - new) + more
         top[index, h] = jnp.broadcast_to(new, (8, BS))
 
 
@@ -158,7 +158,7 @@
         for h in range(HEADS):
             pair = (grid_a[h], grid_b[h])
             new = jnp.maximum(*[jnp.where(u, m, NEG) for u, (_o, m) in zip(used, pair)])
-            first, second = [o * jnp.where(u, jnp.exp(m - new), 0.0) for u, (o, m) in zip(used, pair)]
+            first, second = [jnp.where(u, o * jnp.exp(m - new), 0.0) for u, (o, m) in zip(used, pair)]
             acc[block, h] = first + second
             top[block, h] = jnp.broadcast_to(new, (8, BS))
 
@@ -195,7 +195,7 @@
         for h in range(HEADS):
             o = acc[index, h]
             l = o[HD : HD + 1]
-            value = (o[:HD] * jnp.where(live & (l > 0), 1.0 / jnp.where(l > 0, l, 1.0), 0.0)).astype(jnp.bfloat16)
+            value = jnp.where(live & (l > 0), o[:HD] / jnp.where(l > 0, l, 1.0), 0.0).astype(jnp.bfloat16)
             at = first + h * HD
             mix[chunk, at : at + HD] = value[:, :128]
             mix[chunk + 1, at : at + HD] = value[:, 128:]

time: 44.5 us -> 44.5 us (level)
  no operation moved by 1% of the time
where the time goes in v5:
time: 44.5 us; the launch traced here: 44.1 us
  starting transfers between devices  26.2 us (59%)
  waiting for transfers between devices  8.45 us (19%)
  Pallas kernels  8.16 us (18%)
  between operations  1.33 us (3%)
    all_to_all x1, starting transfers between devices, body(): lax.all_to_all(w_spread, 'head', split_axis=0, concat_axis=0, tiled=True)  9.42 us
    ppermute x1, starting transfers between devices, body(): rec_b = lax.ppermute(pay_b, 'tile', swap_b)  8.14 us
    all_to_all x1, starting transfers between devices, body(): lax.all_to_all(mixes[0], 'head', split_axis=0, concat_axis=0, tiled=True)  4.8 us
    all_to_all x1, waiting for transfers between devices, body(): lax.all_to_all(mixes[0], 'head', split_axis=0, concat_axis=0, tiled=True)  4.01 us
    ppermute x1, waiting for transfers between devices, body(): rec_b = lax.ppermute(pay_b, 'tile', swap_b)  3.82 us
    pallas_call x1, Pallas kernels, body(): pl.pallas_call(project_kernel, out_shape=(pay_shape, pay_b_shape, w_shape...  2.98 us
    pallas_call x1, Pallas kernels, body(): pl.pallas_call(seam_kernel, out_shape=((mix_shape,) * GROUPS if MIX_BY_PE...  2.22 us
    ppermute x1, starting transfers between devices, body(): rec_a = lax.ppermute(pay_a2, 'tile', swap_a)  1.92 us
  transfers between devices with their start and end apart: 5, of which 3 were waited for; matrix products, arithmetic and copies ran while one was open for 0% of the time, Pallas kernels for 9%

profile of v5, /device:TPU:2, one launch (start us, length us, event | category | flops | bytes accessed | tf_op | source)
XLA Modules:
  0.0 44.1 jit_solution(16918805409884940002)
XLA Ops:
  1.3 3.0 %shard_map.122 = (bf16[1168,256]{1,0:T(8,128)(2,1)S(1)}, bf16[1184,256]{1,0:T(8,128)(2,1)S(1)}, bf16[4,192,768]{2,1,0:T(8,128)(2,1)}) custom-call(s32[1]{0:T(128)S(6)} %copy.17.count_any, s32[2]{0:T(128)} %home_hbm.1, s32[2]{0:T(128)} %seam_hbm.1, bf16[512,768]{1,0:T(8,128)(2,1)} %grid.1, bf16[512,768]{1,0:T(8,128)(2,1)} %obs.1, bf16[192,768]{1,0:T(8,128)(2,1)} %bitcast.4, ...), custom_call_target="tpu_custom_call" | custom-call | flops 1 | bytes 1 | tf_op jit(solution)/shard_map/pallas_call | solution.py:265
  4.3 9.4 %all-to-all-start.1 = ((bf16[4,192,768]{2,1,0:T(8,128)(2,1)}), bf16[4,192,768]{2,1,0:T(8,128)(2,1)S(1)}, u32[]{:S(2)}, u32[]{:S(2)}) async-start(bf16[4,192,768]{2,1,0:T(8,128)(2,1)} %get-tuple-element.14), calls=%async_computation.1 | async-start | bytes 2359296 | tf_op jit(solution)/shard_map/all_to_all | solution.py:288
  13.7 8.1 %collective-permute-start.1 = (bf16[1184,256]{1,0:T(8,128)(2,1)S(1)}, bf16[1184,256]{1,0:T(8,128)(2,1)S(1)}, u32[]{:S(2)}, u32[]{:S(2)}) collective-permute-start(bf16[1184,256]{1,0:T(8,128)(2,1)S(1)} %get-tuple-element.10.pay_b), channel_id=1, source_target_pairs={{0,508},{4,8},{8,4},{12,16},{16,12},{20,24},{24,20},{28,32},{32,28... | collective-permute-start | bytes 1818632 | tf_op jit(solution)/shard_map/ppermute | solution.py:289
  21.8 1.9 %collective-permute-start = (bf16[1168,256]{1,0:T(8,128)(2,1)S(1)}, bf16[1168,256]{1,0:T(8,128)(2,1)S(1)}, u32[]{:S(2)}, u32[]{:S(2)}) collective-permute-start(bf16[1168,256]{1,0:T(8,128)(2,1)S(1)} %get-tuple-element.9.pay_a), channel_id=1, source_target_pairs={{0,4},{4,0},{8,12},{12,8},{16,20},{20,16},{24,28},{28,24},{32,36},... | collective-permute-start | bytes 1794056 | tf_op jit(solution)/shard_map/ppermute | solution.py:299
  23.8 1.4 %shard_map.123 = (f32[4,3,80,256]{3,2,1,0:T(8,128)S(1)}, f32[4,3,8,256]{3,2,1,0:T(8,128)S(1)}) custom-call(bf16[1168,256]{1,0:T(8,128)(2,1)S(1)} %get-tuple-element.9.pay_a, bf16[1184,256]{1,0:T(8,128)(2,1)S(1)} %get-tuple-element.10.pay_b), custom_call_target="tpu_custom_call" | custom-call | flops 3000000000 | bytes 1 | tf_op jit(solution)/shard_map/pallas_call | solution.py:290
  25.1 0.6 %collective-permute-done.rec_a = bf16[1168,256]{1,0:T(8,128)(2,1)S(1)} collective-permute-done((bf16[1168,256]{1,0:T(8,128)(2,1)S(1)}, bf16[1168,256]{1,0:T(8,128)(2,1)S(1)}, u32[]{:S(2)}, u32[]{:S(2)}) %collective-permute-start) | collective-permute-done | bytes 598048 | tf_op jit(solution)/shard_map/ppermute | solution.py:299
  25.7 3.8 %collective-permute-done.1.rec_b = bf16[1184,256]{1,0:T(8,128)(2,1)S(1)} collective-permute-done((bf16[1184,256]{1,0:T(8,128)(2,1)S(1)}, bf16[1184,256]{1,0:T(8,128)(2,1)S(1)}, u32[]{:S(2)}, u32[]{:S(2)}) %collective-permute-start.1) | collective-permute-done | bytes 606240 | tf_op jit(solution)/shard_map/ppermute | solution.py:289
  29.6 2.2 %shard_map.124 = (bf16[4,384,128]{2,1,0:T(8,128)(2,1)}, f32[4,3,80,256]{3,2,1,0:T(8,128)S(1)}, f32[4,3,8,256]{3,2,1,0:T(8,128)S(1)}) custom-call(bf16[1168,256]{1,0:T(8,128)(2,1)S(1)} %get-tuple-element.9.pay_a, bf16[1184,256]{1,0:T(8,128)(2,1)S(1)} %get-tuple-element.10.pay_b, ...), custom_call_target="tpu_custom_call", output_to_operand_aliasing={{1}: (4, {}), {2}: (5, {})} | custom-call | flops 1 | bytes 1 | tf_op jit(solution)/shard_map/pallas_call | solution.py:301
  31.8 0.0 all-to-all-done.1.w_own
  31.8 4.8 %all-to-all-start = ((bf16[4,384,128]{2,1,0:T(8,128)(2,1)}), bf16[4,384,128]{2,1,0:T(8,128)(2,1)S(1)}, u32[]{:S(2)}, u32[]{:S(2)}) async-start(bf16[4,384,128]{2,1,0:T(8,128)(2,1)} %get-tuple-element.13), calls=%async_computation | async-start | bytes 786432 | tf_op jit(solution)/shard_map/all_to_all | solution.py:318
  36.6 1.9 %collective-permute-start.2 = (bf16[4,192,768]{2,1,0:T(8,128)(2,1)S(1)}, bf16[4,192,768]{2,1,0:T(8,128)(2,1)S(1)}, u32[]{:S(2)}, u32[]{:S(2)}) collective-permute-start(bf16[4,192,768]{2,1,0:T(8,128)(2,1)S(1)} %all-to-all-done.1.w_own), channel_id=1, source_target_pairs={{0,4},{4,0},{8,12},{12,8},{16,20},{20,16},{24,28},{28,24},{32,36},... | collective-permute-start | bytes 3538952 | tf_op jit(solution)/shard_map/ppermute | solution.py:320
  38.5 4.0 %all-to-all-done.mixes = bf16[4,384,128]{2,1,0:T(8,128)(2,1)S(1)} async-done(((bf16[4,384,128]{2,1,0:T(8,128)(2,1)}), bf16[4,384,128]{2,1,0:T(8,128)(2,1)S(1)}, u32[]{:S(2)}, u32[]{:S(2)}) %all-to-all-start) | async-done | bytes 393248 | tf_op jit(solution)/shard_map/all_to_all | solution.py:318
  42.5 0.4 shard_map.125.own
  42.9 0.0 collective-permute-done.2.w_other
  43.0 1.2 %shard_map.126 = (bf16[128,768]{1,0:T(8,128)(2,1)}, bf16[128,768]{1,0:T(8,128)(2,1)}) custom-call(bf16[4,384,128]{2,1,0:T(8,128)(2,1)S(1)} %all-to-all-done.mixes, bf16[4,192,768]{2,1,0:T(8,128)(2,1)S(1)} %collective-permute-done.2.w_other, bf16[128,768]{1,0:T(8,128)(2,1)S(1)} %shard_map.125.own), custom_call_target="tpu_custom_call" | custom-call | flops 1 | bytes 1 | tf_op jit(solution)/shard_map/pallas_call | solution.py:329
Async XLA Ops:
  4.3 27.5 %all-to-all-start.1 = ((bf16[4,192,768]{2,1,0:T(8,128)(2,1)}), bf16[4,192,768]{2,1,0:T(8,128)(2,1)S(1)}, u32[]{:S(2)}, u32[]{:S(2)}) async-start(bf16[4,192,768]{2,1,0:T(8,128)(2,1)} %get-tuple-element.14), calls=%async_computation.1 | async-start | bytes 2359296 | tf_op jit(solution)/shard_map/all_to_all | solution.py:288
  13.7 15.9 %collective-permute-start.1 = (bf16[1184,256]{1,0:T(8,128)(2,1)S(1)}, bf16[1184,256]{1,0:T(8,128)(2,1)S(1)}, u32[]{:S(2)}, u32[]{:S(2)}) collective-permute-start(bf16[1184,256]{1,0:T(8,128)(2,1)S(1)} %get-tuple-element.10.pay_b), channel_id=1, source_target_pairs={{0,508},{4,8},{8,4},{12,16},{16,12},{20,24},{24,20},{28,32},{32,28... | collective-permute-start | bytes 1818632 | tf_op jit(solution)/shard_map/ppermute | solution.py:289
  21.8 3.9 %collective-permute-start = (bf16[1168,256]{1,0:T(8,128)(2,1)S(1)}, bf16[1168,256]{1,0:T(8,128)(2,1)S(1)}, u32[]{:S(2)}, u32[]{:S(2)}) collective-permute-start(bf16[1168,256]{1,0:T(8,128)(2,1)S(1)} %get-tuple-element.9.pay_a), channel_id=1, source_target_pairs={{0,4},{4,0},{8,12},{12,8},{16,20},{20,16},{24,28},{28,24},{32,36},... | collective-permute-start | bytes 1794056 | tf_op jit(solution)/shard_map/ppermute | solution.py:299
  31.8 10.7 %all-to-all-start = ((bf16[4,384,128]{2,1,0:T(8,128)(2,1)}), bf16[4,384,128]{2,1,0:T(8,128)(2,1)S(1)}, u32[]{:S(2)}, u32[]{:S(2)}) async-start(bf16[4,384,128]{2,1,0:T(8,128)(2,1)} %get-tuple-element.13), calls=%async_computation | async-start | bytes 786432 | tf_op jit(solution)/shard_map/all_to_all | solution.py:318
  36.6 6.4 %collective-permute-start.2 = (bf16[4,192,768]{2,1,0:T(8,128)(2,1)S(1)}, bf16[4,192,768]{2,1,0:T(8,128)(2,1)S(1)}, u32[]{:S(2)}, u32[]{:S(2)}) collective-permute-start(bf16[4,192,768]{2,1,0:T(8,128)(2,1)S(1)} %all-to-all-done.1.w_own), channel_id=1, source_target_pairs={{0,4},{4,0},{8,12},{12,8},{16,20},{20,16},{24,28},{28,24},{32,36},... | collective-permute-start | bytes 3538952 | tf_op jit(solution)/shard_map/ppermute | solution.py:320

commit v6 on v5

--- a/solution.py
+++ b/solution.py
@@ -164,7 +164,7 @@
 
 
 def seam_kernel(pay_a, pay_b, rec_a, rec_b, _acc, _top, *refs):
-    outs, (acc, top, mix) = refs[:-3], refs[-3:]
+    out, acc, top, mix, sems = refs
     tasks, blocks, lives = [], [], []
     lives_own = []
     for pay, rec in zip((pay_a, pay_b), (rec_a, rec_b)):
@@ -183,10 +183,9 @@
             fold(acc, top, blocks[i // 2], parts, lives[i // 2])
         else:
             fold(acc, top, 2 + i // 2, parts, True)
-    if len(outs) == 1:
-        mix = outs[0]
     slot_a, slot_b = slots()
-    for index in range(4):
+    stores = []
+    for index in (2, 3, 0, 1):
         if index < 2:
             chunk, first, live = 2 * index, 0, True
         else:
@@ -199,9 +198,12 @@
             at = first + h * HD
             mix[chunk, at : at + HD] = value[:, :128]
             mix[chunk + 1, at : at + HD] = value[:, 128:]
-    if len(outs) > 1:
-        for s, out in enumerate(outs):
-            out[...] = mix[(lax.axis_index("head") + s) % GROUPS]
+        if index in (3, 1):
+            part = (slice(None), pl.ds(first, WIDTH))
+            stores.append(pltpu.make_async_copy(mix.at[part], out.at[part], sems.at[len(stores)]))
+            stores[-1].start()
+    for copy in stores:
+        copy.wait()
 
 
 def apply_out(mixes, first, w):
@@ -258,7 +260,7 @@
     acc_shape = pltpu.VMEM((4, HEADS, ROWS_O, BS), f32)
     top_shape = pltpu.VMEM((4, HEADS, 8, BS), f32)
     mix_shape = jax.ShapeDtypeStruct((PAIR, 128), bf16)
-    mixes_shape = pltpu.VMEM((GROUPS, PAIR, 128), bf16)
+    mixes_shape = pltpu.HBM((GROUPS, PAIR, 128), bf16)
     w_shape = pltpu.HBM((GROUPS, WIDTH, D), bf16)
     out_shape = jax.ShapeDtypeStruct((128, D), bf16)
 
@@ -302,9 +304,9 @@
         seam_kernel,
         out_shape=((mix_shape,) * GROUPS if MIX_BY_PERMUTE else (mixes_shape,)) + (acc_shape, top_shape),
         in_specs=[VMEM] * 6,
-        out_specs=(VMEM,) * (count + 2),
+        out_specs=(ANY,) + (VMEM,) * 2,
         input_output_aliases={4: count, 5: count + 1},
-        scratch_shapes=[pltpu.VMEM(mixes_shape.shape if MIX_BY_PERMUTE else (1, 16, 128), bf16)],
+        scratch_shapes=[pltpu.VMEM(mixes_shape.shape, bf16), pltpu.SemaphoreType.DMA((2,))],
         compiler_params=PARAMS,
         cost_estimate=cost(1, 1),
     )(pay_a, pay_b, in_vmem(rec_a), in_vmem(rec_b), acc, top)

time: 44.5 us -> 44.5 us (level)
  no operation moved by 1% of the time
where the time goes in v6:
time: 44.5 us; the launch traced here: 44.1 us
  starting transfers between devices  26.2 us (59%)
  waiting for transfers between devices  8.45 us (19%)
  Pallas kernels  8.14 us (18%)
  between operations  1.35 us (3%)
    all_to_all x1, starting transfers between devices, body(): lax.all_to_all(w_spread, 'head', split_axis=0, concat_axis=0, tiled=True)  9.42 us
    ppermute x1, starting transfers between devices, body(): rec_b = lax.ppermute(pay_b, 'tile', swap_b)  8.14 us
    all_to_all x1, starting transfers between devices, body(): lax.all_to_all(mixes[0], 'head', split_axis=0, concat_axis=0, tiled=True)  4.81 us
    all_to_all x1, waiting for transfers between devices, body(): lax.all_to_all(mixes[0], 'head', split_axis=0, concat_axis=0, tiled=True)  4.01 us
    ppermute x1, waiting for transfers between devices, body(): rec_b = lax.ppermute(pay_b, 'tile', swap_b)  3.82 us
    pallas_call x1, Pallas kernels, body(): pl.pallas_call(project_kernel, out_shape=(pay_shape, pay_b_shape, w_shape...  2.98 us
    pallas_call x1, Pallas kernels, body(): pl.pallas_call(seam_kernel, out_shape=((mix_shape,) * GROUPS if MIX_BY_PE...  2.19 us
    ppermute x1, starting transfers between devices, body(): rec_a = lax.ppermute(pay_a2, 'tile', swap_a)  1.92 us
  transfers between devices with their start and end apart: 5, of which 3 were waited for; matrix products, arithmetic and copies ran while one was open for 0% of the time, Pallas kernels for 9%

profile of v6, /device:TPU:2, one launch (start us, length us, event | category | flops | bytes accessed | tf_op | source)
XLA Modules:
  0.0 44.1 jit_solution(10662469019688782304)
XLA Ops:
  1.3 3.0 %shard_map.122 = (bf16[1168,256]{1,0:T(8,128)(2,1)S(1)}, bf16[1184,256]{1,0:T(8,128)(2,1)S(1)}, bf16[4,192,768]{2,1,0:T(8,128)(2,1)}) custom-call(s32[1]{0:T(128)S(6)} %copy.17.count_any, s32[2]{0:T(128)} %home_hbm.1, s32[2]{0:T(128)} %seam_hbm.1, bf16[512,768]{1,0:T(8,128)(2,1)} %grid.1, bf16[512,768]{1,0:T(8,128)(2,1)} %obs.1, bf16[192,768]{1,0:T(8,128)(2,1)} %bitcast.4, ...), custom_call_target="tpu_custom_call" | custom-call | flops 1 | bytes 1 | tf_op jit(solution)/shard_map/pallas_call | solution.py:267
  4.3 9.4 %all-to-all-start.1 = ((bf16[4,192,768]{2,1,0:T(8,128)(2,1)}), bf16[4,192,768]{2,1,0:T(8,128)(2,1)S(1)}, u32[]{:S(2)}, u32[]{:S(2)}) async-start(bf16[4,192,768]{2,1,0:T(8,128)(2,1)} %get-tuple-element.14), calls=%async_computation.1 | async-start | bytes 2359296 | tf_op jit(solution)/shard_map/all_to_all | solution.py:290
  13.7 8.1 %collective-permute-start.1 = (bf16[1184,256]{1,0:T(8,128)(2,1)S(1)}, bf16[1184,256]{1,0:T(8,128)(2,1)S(1)}, u32[]{:S(2)}, u32[]{:S(2)}) collective-permute-start(bf16[1184,256]{1,0:T(8,128)(2,1)S(1)} %get-tuple-element.10.pay_b), channel_id=1, source_target_pairs={{0,508},{4,8},{8,4},{12,16},{16,12},{20,24},{24,20},{28,32},{32,28... | collective-permute-start | bytes 1818632 | tf_op jit(solution)/shard_map/ppermute | solution.py:291
  21.8 1.9 %collective-permute-start = (bf16[1168,256]{1,0:T(8,128)(2,1)S(1)}, bf16[1168,256]{1,0:T(8,128)(2,1)S(1)}, u32[]{:S(2)}, u32[]{:S(2)}) collective-permute-start(bf16[1168,256]{1,0:T(8,128)(2,1)S(1)} %get-tuple-element.9.pay_a), channel_id=1, source_target_pairs={{0,4},{4,0},{8,12},{12,8},{16,20},{20,16},{24,28},{28,24},{32,36},... | collective-permute-start | bytes 1794056 | tf_op jit(solution)/shard_map/ppermute | solution.py:301
  23.8 1.4 %shard_map.123 = (f32[4,3,80,256]{3,2,1,0:T(8,128)S(1)}, f32[4,3,8,256]{3,2,1,0:T(8,128)S(1)}) custom-call(bf16[1168,256]{1,0:T(8,128)(2,1)S(1)} %get-tuple-element.9.pay_a, bf16[1184,256]{1,0:T(8,128)(2,1)S(1)} %get-tuple-element.10.pay_b), custom_call_target="tpu_custom_call" | custom-call | flops 3000000000 | bytes 1 | tf_op jit(solution)/shard_map/pallas_call | solution.py:292
  25.1 0.6 %collective-permute-done.rec_a = bf16[1168,256]{1,0:T(8,128)(2,1)S(1)} collective-permute-done((bf16[1168,256]{1,0:T(8,128)(2,1)S(1)}, bf16[1168,256]{1,0:T(8,128)(2,1)S(1)}, u32[]{:S(2)}, u32[]{:S(2)}) %collective-permute-start) | collective-permute-done | bytes 598048 | tf_op jit(solution)/shard_map/ppermute | solution.py:301
  25.7 3.8 %collective-permute-done.1.rec_b = bf16[1184,256]{1,0:T(8,128)(2,1)S(1)} collective-permute-done((bf16[1184,256]{1,0:T(8,128)(2,1)S(1)}, bf16[1184,256]{1,0:T(8,128)(2,1)S(1)}, u32[]{:S(2)}, u32[]{:S(2)}) %collective-permute-start.1) | collective-permute-done | bytes 606240 | tf_op jit(solution)/shard_map/ppermute | solution.py:291
  29.6 2.2 %shard_map.124 = (bf16[4,384,128]{2,1,0:T(8,128)(2,1)}, f32[4,3,80,256]{3,2,1,0:T(8,128)S(1)}, f32[4,3,8,256]{3,2,1,0:T(8,128)S(1)}) custom-call(bf16[1168,256]{1,0:T(8,128)(2,1)S(1)} %get-tuple-element.9.pay_a, bf16[1184,256]{1,0:T(8,128)(2,1)S(1)} %get-tuple-element.10.pay_b, ...), custom_call_target="tpu_custom_call", output_to_operand_aliasing={{1}: (4, {}), {2}: (5, {})} | custom-call | flops 1 | bytes 1 | tf_op jit(solution)/shard_map/pallas_call | solution.py:303
  31.8 0.0 all-to-all-done.1.w_own
  31.8 4.8 %all-to-all-start = ((bf16[4,384,128]{2,1,0:T(8,128)(2,1)}), bf16[4,384,128]{2,1,0:T(8,128)(2,1)S(1)}, u32[]{:S(2)}, u32[]{:S(2)}) async-start(bf16[4,384,128]{2,1,0:T(8,128)(2,1)} %get-tuple-element.13), calls=%async_computation | async-start | bytes 786432 | tf_op jit(solution)/shard_map/all_to_all | solution.py:320
  36.6 1.9 %collective-permute-start.2 = (bf16[4,192,768]{2,1,0:T(8,128)(2,1)S(1)}, bf16[4,192,768]{2,1,0:T(8,128)(2,1)S(1)}, u32[]{:S(2)}, u32[]{:S(2)}) collective-permute-start(bf16[4,192,768]{2,1,0:T(8,128)(2,1)S(1)} %all-to-all-done.1.w_own), channel_id=1, source_target_pairs={{0,4},{4,0},{8,12},{12,8},{16,20},{20,16},{24,28},{28,24},{32,36},... | collective-permute-start | bytes 3538952 | tf_op jit(solution)/shard_map/ppermute | solution.py:322
  38.5 4.0 %all-to-all-done.mixes = bf16[4,384,128]{2,1,0:T(8,128)(2,1)S(1)} async-done(((bf16[4,384,128]{2,1,0:T(8,128)(2,1)}), bf16[4,384,128]{2,1,0:T(8,128)(2,1)S(1)}, u32[]{:S(2)}, u32[]{:S(2)}) %all-to-all-start) | async-done | bytes 393248 | tf_op jit(solution)/shard_map/all_to_all | solution.py:320
  42.5 0.4 shard_map.125.own
  42.9 0.0 collective-permute-done.2.w_other
  43.0 1.2 %shard_map.126 = (bf16[128,768]{1,0:T(8,128)(2,1)}, bf16[128,768]{1,0:T(8,128)(2,1)}) custom-call(bf16[4,384,128]{2,1,0:T(8,128)(2,1)S(1)} %all-to-all-done.mixes, bf16[4,192,768]{2,1,0:T(8,128)(2,1)S(1)} %collective-permute-done.2.w_other, bf16[128,768]{1,0:T(8,128)(2,1)S(1)} %shard_map.125.own), custom_call_target="tpu_custom_call" | custom-call | flops 1 | bytes 1 | tf_op jit(solution)/shard_map/pallas_call | solution.py:331
Async XLA Ops:
  4.3 27.5 %all-to-all-start.1 = ((bf16[4,192,768]{2,1,0:T(8,128)(2,1)}), bf16[4,192,768]{2,1,0:T(8,128)(2,1)S(1)}, u32[]{:S(2)}, u32[]{:S(2)}) async-start(bf16[4,192,768]{2,1,0:T(8,128)(2,1)} %get-tuple-element.14), calls=%async_computation.1 | async-start | bytes 2359296 | tf_op jit(solution)/shard_map/all_to_all | solution.py:290
  13.7 15.9 %collective-permute-start.1 = (bf16[1184,256]{1,0:T(8,128)(2,1)S(1)}, bf16[1184,256]{1,0:T(8,128)(2,1)S(1)}, u32[]{:S(2)}, u32[]{:S(2)}) collective-permute-start(bf16[1184,256]{1,0:T(8,128)(2,1)S(1)} %get-tuple-element.10.pay_b), channel_id=1, source_target_pairs={{0,508},{4,8},{8,4},{12,16},{16,12},{20,24},{24,20},{28,32},{32,28... | collective-permute-start | bytes 1818632 | tf_op jit(solution)/shard_map/ppermute | solution.py:291
  21.8 3.9 %collective-permute-start = (bf16[1168,256]{1,0:T(8,128)(2,1)S(1)}, bf16[1168,256]{1,0:T(8,128)(2,1)S(1)}, u32[]{:S(2)}, u32[]{:S(2)}) collective-permute-start(bf16[1168,256]{1,0:T(8,128)(2,1)S(1)} %get-tuple-element.9.pay_a), channel_id=1, source_target_pairs={{0,4},{4,0},{8,12},{12,8},{16,20},{20,16},{24,28},{28,24},{32,36},... | collective-permute-start | bytes 1794056 | tf_op jit(solution)/shard_map/ppermute | solution.py:301
  31.8 10.7 %all-to-all-start = ((bf16[4,384,128]{2,1,0:T(8,128)(2,1)}), bf16[4,384,128]{2,1,0:T(8,128)(2,1)S(1)}, u32[]{:S(2)}, u32[]{:S(2)}) async-start(bf16[4,384,128]{2,1,0:T(8,128)(2,1)} %get-tuple-element.13), calls=%async_computation | async-start | bytes 786432 | tf_op jit(solution)/shard_map/all_to_all | solution.py:320
  36.6 6.4 %collective-permute-start.2 = (bf16[4,192,768]{2,1,0:T(8,128)(2,1)S(1)}, bf16[4,192,768]{2,1,0:T(8,128)(2,1)S(1)}, u32[]{:S(2)}, u32[]{:S(2)}) collective-permute-start(bf16[4,192,768]{2,1,0:T(8,128)(2,1)S(1)} %all-to-all-done.1.w_own), channel_id=1, source_target_pairs={{0,4},{4,0},{8,12},{12,8},{16,20},{20,16},{24,28},{28,24},{32,36},... | collective-permute-start | bytes 3538952 | tf_op jit(solution)/shard_map/ppermute | solution.py:322
